TPU v7x, 512 devices: a whole 4x8x8 slice. The times are simulated.
512 devices in a mesh: lat: 128 (over z, y, core), ch: 4 (over x).
Axes of the slice: x: 4, y: 8, z: 8, core: 2. Of those that a mesh axis runs over, the one named last changes fastest.
Arguments:
- grid_field: bfloat16 [256, 512, 1440], P('ch', 'lat'), may hold values from -6 to 6
- order_slots: int32 [512], replicated, may hold values from 0 to 511, each once
- mix_weight: bfloat16 [256, 256], replicated, may hold values from -0.375 to 0.375
- degree_gain: float32 [256, 512], P('ch'), may hold values from 0.3 to 3
- cotangent: bfloat16 [256, 512, 1440], P('ch', 'lat'), may hold values from -6 to 6
Outputs:
- block_output: bfloat16 [256, 512, 1440], P('ch', 'lat')
- spectrum: bfloat16 [512, 2, 256, 512], P('lat', None, 'ch')
- grad_field: bfloat16 [256, 512, 1440], P('ch', 'lat')
- grad_mix: float32 [256, 256], P(None, 'ch')
- grad_gain: float32 [256, 512], P('ch')
Inputs may be any that keep to these rules, and one draw needn't show every extreme that they name: `order_slots`: each order from 0 to 511 stands in exactly one slot.
All inputs are finite; a program needn't handle non-finite values.
Results may differ from a plain program's by a relative error of at most 0.02.
Values may be sent and summed in bfloat16 or wider, within the bound.
A program may use at most 128 MiB of HBM per device.

v0:
```python
import math

import jax
import jax.numpy as jnp
from jax import lax
from jax.sharding import PartitionSpec as P

renew_every = 32


def lat_angles(lat_count):
    rows = jnp.arange(lat_count, dtype=jnp.int32).astype(jnp.float32)
    theta = math.pi * (rows + 0.5) / lat_count
    return (jnp.cos(theta), jnp.sin(theta))


def long_table(order_slots, lon_count):
    points = jnp.arange(lon_count, dtype=jnp.int32)
    wrapped = points[:, None] * order_slots[None, :] % lon_count
    angle = wrapped.astype(jnp.float32) * (2.0 * math.pi / lon_count)
    factor = math.sqrt(2.0 / lon_count)
    table = jnp.stack([jnp.cos(angle) * factor, -jnp.sin(angle) * factor], axis=-1)
    forward_tab = table.reshape(lon_count, -1).astype(jnp.bfloat16)
    halving = jnp.where(order_slots == 0, 0.5, 1.0).astype(jnp.float32)
    halving_cols = jnp.repeat(halving, 2)
    return (forward_tab, halving_cols)


def legendre_rows(own_orders, lat_count, mode_count):
    cosines, lat_sines = lat_angles(lat_count)
    order_vals = own_orders.astype(jnp.float32)
    counter = jnp.arange(1, mode_count, dtype=jnp.int32).astype(jnp.float32)
    ratios = jnp.log((2.0 * counter - 1.0) / (2.0 * counter))
    partial_logs = jnp.concatenate([jnp.zeros((1,), jnp.float32), jnp.cumsum(ratios)])
    matches = jnp.arange(mode_count, dtype=jnp.int32)[None, :] == own_orders[:, None]
    picked = jnp.sum(jnp.where(matches, partial_logs[None, :], 0.0), axis=1)
    log_start = (
        0.5 * (jnp.log(order_vals + 0.5) + picked)[:, None]
        + order_vals[:, None] * jnp.log(lat_sines)[None, :]
    )
    order_col = order_vals[:, None]

    def advance(carry, unused):
        previous, current, scale, base = carry
        factor = jnp.exp(0.5 * scale)
        columns = []
        for offset in range(renew_every):
            columns.append(current)
            degree = order_col + (base + offset + 1).astype(jnp.float32)
            upper = jnp.sqrt(
                (4.0 * degree * degree - 1.0) / (degree * degree - order_col * order_col)
            )
            below = degree - 1.0
            lower = jnp.sqrt(
                (below * below - order_col * order_col)
                / jnp.maximum(4.0 * below * below - 1.0, 1.0)
            )
            following = upper * (cosines[None, :] * current - lower * previous)
            previous, current = (current, following)
        stacked = jnp.stack(columns, axis=-1) * factor[:, :, None] * factor[:, :, None]
        biggest = jnp.maximum(jnp.abs(previous), jnp.abs(current))
        shift = jnp.log(biggest)
        rescale = jnp.exp(-shift)
        return ((previous * rescale, current * rescale, scale + shift, base + renew_every), stacked)

    block_count = -(-mode_count // renew_every)
    start = (
        jnp.zeros_like(log_start),
        jnp.ones_like(log_start),
        log_start,
        jnp.zeros((), jnp.int32),
    )
    final_carry, pieces = lax.scan(advance, start, None, length=block_count)
    values = jnp.transpose(pieces, (1, 2, 0, 3)).reshape(own_orders.shape[0], lat_count, -1)[
        :, :, :mode_count
    ]
    live = jnp.arange(mode_count, dtype=jnp.int32)[None, :] < (mode_count - own_orders)[:, None]
    scaled = jnp.where(live[:, None, :], values, 0.0) * math.sqrt(math.pi / lat_count)
    return scaled.astype(jnp.bfloat16)


def gain_lookup(degree_gain, own_orders):
    padded = jnp.concatenate([degree_gain, jnp.zeros_like(degree_gain)], axis=1)

    def pick_rows(first):
        return lax.dynamic_slice_in_dim(padded, first, degree_gain.shape[1], 1)

    return jax.vmap(pick_rows)(own_orders)


def degree_sum(terms, own_orders):
    mode_count = terms.shape[2]
    padded = jnp.concatenate([jnp.zeros_like(terms), terms], axis=2)

    def place(row, order_value):
        return lax.dynamic_slice_in_dim(row, mode_count - order_value, mode_count, 1)

    return jnp.sum(jax.vmap(place)(padded, own_orders), axis=0)


def gelu_value(values):
    return values * 0.5 * (1.0 + lax.erf(values * (1.0 / math.sqrt(2.0))))


def gelu_slope(values):
    normal_cdf = 0.5 * (1.0 + lax.erf(values * (1.0 / math.sqrt(2.0))))
    return normal_cdf + values * jnp.exp(-0.5 * values * values) * (1.0 / math.sqrt(2.0 * math.pi))


def to_orders(values):
    return lax.all_to_all(values, "lat", split_axis=2, concat_axis=2, tiled=True)


def to_latitudes(values):
    return lax.all_to_all(values, "lat", split_axis=2, concat_axis=2, tiled=True)


def body(grid_field, order_slots, mix_weight, degree_gain, cotangent):
    chan_local, lat_local, lon_count = grid_field.shape
    mode_count = order_slots.shape[0]
    lat_devices = lax.axis_size("lat")
    orders_local = mode_count // lat_devices
    lat_count = lat_local * lat_devices
    own_lat = lax.axis_index("lat")
    own_chan = lax.axis_index("ch")
    forward_tab, halving_cols = long_table(order_slots, lon_count)
    cosines, lat_sines = lat_angles(lat_count)
    band_sines = lax.dynamic_slice_in_dim(lat_sines, own_lat * lat_local, lat_local)
    own_orders = lax.dynamic_slice_in_dim(order_slots, own_lat * orders_local, orders_local)
    legendre = legendre_rows(own_orders, lat_count, mode_count)
    legendre_blocks = legendre.reshape(orders_local, lat_devices, lat_local, mode_count)
    gain_rows = gain_lookup(degree_gain, own_orders)
    spectral = jnp.einsum(
        "cjn,nq->cjq", grid_field, forward_tab, preferred_element_type=jnp.float32
    )
    spectral = (spectral * band_sines[None, :, None]).astype(jnp.bfloat16)
    received = to_orders(spectral).reshape(chan_local, lat_local, lat_devices, orders_local, 2)
    coeffs = jnp.einsum(
        "cjesr,sejk->srck", received, legendre_blocks, preferred_element_type=jnp.float32
    )
    coeffs = coeffs.astype(jnp.bfloat16)
    all_inputs = lax.all_gather(coeffs, "ch", axis=2, tiled=True)
    weight_cols = lax.dynamic_slice_in_dim(mix_weight, own_chan * chan_local, chan_local, 1)
    mixed_pre = jnp.einsum(
        "srik,io->srok", all_inputs, weight_cols, preferred_element_type=jnp.float32
    )
    mixed_pre = mixed_pre.astype(jnp.bfloat16)
    spectrum = (mixed_pre.astype(jnp.float32) * gain_rows[:, None]).astype(jnp.bfloat16)
    returned = jnp.einsum(
        "srck,sejk->cjesr", spectrum, legendre_blocks, preferred_element_type=jnp.float32
    )
    returned = returned.astype(jnp.bfloat16).reshape(chan_local, lat_local, 2 * mode_count)
    grid_side = to_latitudes(returned)
    grid_side = grid_side * halving_cols.astype(jnp.bfloat16)[None, None, :]
    inner_sum = jnp.einsum(
        "cjq,nq->cjn", grid_side, forward_tab, preferred_element_type=jnp.float32
    )
    block_output = (grid_field.astype(jnp.float32) + gelu_value(inner_sum)).astype(jnp.bfloat16)
    slope_grad = (cotangent.astype(jnp.float32) * gelu_slope(inner_sum)).astype(jnp.bfloat16)
    returned_grad = jnp.einsum(
        "cjn,nq->cjq", slope_grad, forward_tab, preferred_element_type=jnp.float32
    )
    returned_grad = (returned_grad * halving_cols[None, None, :]).astype(jnp.bfloat16)
    grad_received = to_orders(returned_grad).reshape(
        chan_local, lat_local, lat_devices, orders_local, 2
    )
    spec_grad = jnp.einsum(
        "cjesr,sejk->srck", grad_received, legendre_blocks, preferred_element_type=jnp.float32
    )
    pre_grad = (spec_grad * gain_rows[:, None]).astype(jnp.bfloat16)
    gain_part = degree_sum(jnp.sum(spec_grad * mixed_pre.astype(jnp.float32), axis=1), own_orders)
    mix_part = jnp.einsum("srik,srok->io", all_inputs, pre_grad, preferred_element_type=jnp.float32)
    weight_rows = lax.dynamic_slice_in_dim(mix_weight, own_chan * chan_local, chan_local, 0)
    coeff_grad = jnp.einsum(
        "srok,io->srik",
        lax.all_gather(pre_grad, "ch", axis=2, tiled=True),
        weight_rows,
        preferred_element_type=jnp.float32,
    ).astype(jnp.bfloat16)
    mix_total, gain_total = lax.psum((mix_part, gain_part), "lat")
    grad_mix = mix_total / mode_count
    grad_gain = gain_total / math.sqrt(mode_count)
    sine_grid = lat_sines.reshape(lat_devices, lat_local).T
    spectral_grad = jnp.einsum(
        "srck,sejk->cjesr", coeff_grad, legendre_blocks, preferred_element_type=jnp.float32
    )
    spectral_grad = (spectral_grad * sine_grid[None, :, :, None, None]).astype(jnp.bfloat16)
    spectral_grad = spectral_grad.reshape(chan_local, lat_local, 2 * mode_count)
    grid_grad = to_latitudes(spectral_grad)
    field_term = jnp.einsum(
        "cjq,nq->cjn", grid_grad, forward_tab, preferred_element_type=jnp.float32
    )
    grad_field = (cotangent.astype(jnp.float32) + field_term).astype(jnp.bfloat16)
    return (block_output, spectrum, grad_field, grad_mix, grad_gain)


def solution(mesh):
    placed = (P("ch", "lat", None), P(), P(), P("ch", None), P("ch", "lat", None))
    return jax.shard_map(
        body,
        mesh=mesh,
        in_specs=placed,
        out_specs=(
            P("ch", "lat", None),
            P("lat", None, "ch", None),
            P("ch", "lat", None),
            P(None, "ch"),
            P("ch", None),
        ),
        check_vma=False,
    )
```

profile of v0, /device:TPU:1, one launch (start us, length us, event | category | flops | bytes accessed | tf_op | source)
XLA Modules:
  0.0 548.9 jit_solution(8339402937956982221)
XLA Ops:
  7.2 13.5 %multiply_convert_fusion.1 = (bf16[1440,512,1]{1,0,2:T(8,128)(2,1)S(1)}, bf16[1440,512,1]{1,0,2:T(8,128)(2,1)S(1)}) fusion(s32[512]{0:T(512)} %param.8), kind=kLoop, calls=%fused_computation.510 | loop fusion | flops 10321920 | bytes 2951168 | tf_op jit(solution)/shard_map/convert.1
  21.1 6.2 %copy.112 = bf16[1440,512,2]{0,2,1:T(2,128)(2,1)} copy(bf16[1440,512,2]{1,0,2:T(8,128)(2,1)S(1)} %pad_maximum_fusion) | data formatting | bytes 5898240 | tf_op jit(solution)/shard_map/stack | solution.py:22
  27.3 6.3 %convert_element_type.534 = bf16[1440,1024]{0,1:T(8,128)(2,1)S(1)} reshape(bf16[1440,512,2]{0,2,1:T(2,128)(2,1)} %copy.112) | data formatting | bytes 5898240 | tf_op jit(solution)/shard_map/convert_element_type | solution.py:23
  33.7 3.5 fusion.340
  37.3 2.3 copy.115
  39.6 3.3 reshape.2542
  42.9 18.9 %all-to-all-start = ((bf16[128,2,1024]{2,1,0:T(2,128)(2,1)}), bf16[128,2,1024]{2,1,0:T(2,128)(2,1)}, u32[]{:S(2)}, u32[]{:S(2)}) async-start(bf16[128,2,1024]{2,1,0:T(2,128)(2,1)} %reshape.2542), calls=%async_computation | async-start | bytes 1048576 | tf_op jit(solution)/shard_map/all_to_all | solution.py:111
  63.2 58.6 %while.26 = (s32[]{:T(128)}, f32[4,512]{1,0:T(4,128)S(1)}, f32[4,512]{1,0:T(4,128)S(1)}, f32[4,512]{1,0:T(4,128)S(1)}, f32[16,4,512,32]{2,1,3,0:T(4,128)}, /*ind...) while((s32[]{:T(128)}, f32[4,512]{1,0:T(4,128)S(1)}, ...), condition=%wide.region_4.5_spmd.clone.clone, body=%wide.region_3.4_spmd.clone.clone.sunk | while | flops 673219 | bytes 1720048 | solution.py:73
  121.8 10.7 %copy.109 = f32[4,512,16,32]{3,2,1,0:T(8,128)} copy(f32[4,512,16,32]{1,0,3,2:T(4,128)} %bitcast.1007) | data formatting | bytes 8388608 | tf_op jit(solution)/shard_map/transpose | solution.py:74
  132.4 13.0 %reshape.2493 = f32[4,128,4,512]{3,2,1,0:T(4,128)} reshape(f32[4,512,16,32]{3,2,1,0:T(8,128)} %copy.109) | data formatting | bytes 8388608 | tf_op jit(solution)/shard_map/reshape | solution.py:74
  145.5 3.7 fusion.263
  149.2 2.7 reshape.2543
  152.0 1.5 fusion.334
  153.5 5.4 while.25
  159.0 31.6 %all-gather.3.cloned.1.call-done = bf16[4,2,256,512]{3,2,1,0:T(8,128)(2,1)} async-done(((bf16[4,2,64,512]{3,2,1,0:T(8,128)(2,1)}), bf16[4,2,256,512]{3,2,1,0:T(8,128)(2,1)}) %all-gather.3.cloned.1.call-update) | async-done | bytes 2097168 | tf_op jit(solution)/shard_map/all_gather | solution.py:142
  190.6 3.2 multiply_convert_fusion.3
  193.7 0.8 copy-done.5
  194.5 1.6 fusion.337
  196.1 2.4 copy.118
  198.5 1.8 copy.189
  200.3 3.3 reshape.2544
  203.7 14.7 %all-to-all-start.1 = ((bf16[128,2,1024]{2,1,0:T(2,128)(2,1)}), bf16[128,2,1024]{2,1,0:T(2,128)(2,1)}, u32[]{:S(2)}, u32[]{:S(2)}) async-start(bf16[128,2,1024]{2,1,0:T(2,128)(2,1)} %reshape.2544), calls=%async_computation.1 | async-start | bytes 1048576 | tf_op jit(solution)/shard_map/all_to_all | solution.py:115
  218.8 19.9 %all-to-all-done.1 = bf16[128,2,1024]{2,1,0:T(2,128)(2,1)} async-done(((bf16[128,2,1024]{2,1,0:T(2,128)(2,1)}), bf16[128,2,1024]{2,1,0:T(2,128)(2,1)}, u32[]{:S(2)}, u32[]{:S(2)}) %all-to-all-start.1) | async-done | bytes 524320 | tf_op jit(solution)/shard_map/all_to_all | solution.py:115
  238.7 2.7 reshape.2545
  241.4 1.3 copy.120
  242.7 4.4 add_convert_fusion
  247.1 2.1 fusion.316
  249.2 1.6 copy.124
  250.8 1.4 reshape.2546
  252.2 26.7 %all_to_all.20 = bf16[128,2,1024]{2,1,0:T(2,128)(2,1)} all-to-all(bf16[128,2,1024]{2,1,0:T(2,128)(2,1)} %reshape.2546), channel_id=1, replica_groups=mesh['lat'=128,'ch'=4] {'lat'}, dimensions={0} | all-to-all | bytes 1048576 | tf_op jit(solution)/shard_map/all_to_all | solution.py:111
  279.0 3.5 reshape.2547
  282.4 3.7 multiply_reduce_fusion
  286.3 27.5 %all-gather.5.cloned.1.call-done = bf16[4,2,256,512]{3,2,1,0:T(8,128)(2,1)} async-done(((bf16[4,2,64,512]{3,2,1,0:T(8,128)(2,1)}), bf16[4,2,256,512]{3,2,1,0:T(8,128)(2,1)}) %all-gather.5.cloned.1.call-update) | async-done | bytes 2097168 | tf_op jit(solution)/shard_map/all_gather | solution.py:176
  313.8 2.8 fusion.325
  316.6 0.8 copy.127
  317.4 0.8 copy.188
  318.2 1.4 reshape.2548
  319.6 14.7 %all-to-all-start.3 = ((bf16[128,2,1024]{2,1,0:T(2,128)(2,1)}), bf16[128,2,1024]{2,1,0:T(2,128)(2,1)}, u32[]{:S(2)}, u32[]{:S(2)}) async-start(bf16[128,2,1024]{2,1,0:T(2,128)(2,1)} %reshape.2548), calls=%async_computation.3 | async-start | bytes 1048576 | tf_op jit(solution)/shard_map/all_to_all | solution.py:115
  335.4 3.0 gather_fusion
  338.4 1.4 reduce_sum.29
  339.8 3.1 fusion.343
  342.9 2.8 copy.134
  345.7 185.6 %all-reduce.8.cloned.1.call-done = (f32[256,64]{0,1:T(8,128)}, f32[64,512]{0,1:T(8,128)}) async-done(((f32[256,64]{0,1:T(8,128)}, f32[64,512]{0,1:T(8,128)}), (f32[256,64]{0,1:T(8,128)}, f32[64,512]{0,1:T(8,128)})) %all-reduce.8.cloned.1.call-update) | async-done | bytes 196624 | tf_op jit(solution)/shard_map/psum | solution.py:180
  531.2 1.0 broadcast_multiply_fusion
  533.0 1.5 broadcast_multiply_fusion.1
  534.5 3.5 reshape.2549
  537.9 2.4 fusion.280
  540.4 1.5 copy.135
  (665 shorter events, 67.4 us)
Async XLA Ops:
  7.2 183.4 %copy-start = (bf16[256,256]{1,0:T(8,128)(2,1)S(1)}, bf16[256,256]{1,0:T(8,128)(2,1)}, u32[]{:S(2)}) copy-start(bf16[256,256]{1,0:T(8,128)(2,1)} %param.9) | copy-start | bytes 393220
  33.6 3.6 copy-start.1
  37.3 24.8 %copy-start.10 = (s32[512]{0:T(512)S(1)}, s32[512]{0:T(512)}, u32[]{:S(2)}) copy-start(s32[512]{0:T(512)} %param.8) | copy-start | bytes 6148
  42.9 106.3 %all-to-all-start = ((bf16[128,2,1024]{2,1,0:T(2,128)(2,1)}), bf16[128,2,1024]{2,1,0:T(2,128)(2,1)}, u32[]{:S(2)}, u32[]{:S(2)}) async-start(bf16[128,2,1024]{2,1,0:T(2,128)(2,1)} %reshape.2542), calls=%async_computation | async-start | bytes 1048576 | tf_op jit(solution)/shard_map/all_to_all | solution.py:111
  61.8 128.8 %all-gather.3.cloned.1.call-start = ((), (), s32[]{:S(2)}) async-start(), calls=%async_computation.4 | async-start | bytes 2621440 | tf_op jit(solution)/shard_map/all_gather | solution.py:142
  152.0 1.5 copy-start.9
  159.0 34.8 %copy-start.7 = (f32[4,64,512]{2,1,0:T(8,128)}, f32[4,64,512]{2,1,0:T(8,128)S(1)}, u32[]{:S(2)}) copy-start(f32[4,64,512]{2,1,0:T(8,128)S(1)} %get-tuple-element.562) | copy-start | bytes 1572868
  193.7 0.8 copy-start.5
  203.7 35.0 %all-to-all-start.1 = ((bf16[128,2,1024]{2,1,0:T(2,128)(2,1)}), bf16[128,2,1024]{2,1,0:T(2,128)(2,1)}, u32[]{:S(2)}, u32[]{:S(2)}) async-start(bf16[128,2,1024]{2,1,0:T(2,128)(2,1)} %reshape.2544), calls=%async_computation.1 | async-start | bytes 1048576 | tf_op jit(solution)/shard_map/all_to_all | solution.py:115
  218.4 95.4 %all-gather.5.cloned.1.call-start = ((), (), s32[]{:S(2)}) async-start(), calls=%async_computation.5 | async-start | bytes 2621440 | tf_op jit(solution)/shard_map/all_gather | solution.py:176
  242.7 4.4 copy-start.2
  242.7 4.4 copy-start.8
  252.2 30.2 %copy-start.4 = (f32[4,2,64,512]{3,2,1,0:T(8,128)S(1)}, f32[4,2,64,512]{3,2,1,0:T(8,128)}, u32[]{:S(2)}) copy-start(f32[4,2,64,512]{3,2,1,0:T(8,128)} %get-tuple-element.805) | copy-start | bytes 3145732
  318.2 16.5 %copy-start.6 = (f32[4,64,512]{2,1,0:T(8,128)S(1)}, f32[4,64,512]{2,1,0:T(8,128)}, u32[]{:S(2)}) copy-start(f32[4,64,512]{2,1,0:T(8,128)} %get-tuple-element.794) | copy-start | bytes 1572868
  319.6 214.9 %all-to-all-start.3 = ((bf16[128,2,1024]{2,1,0:T(2,128)(2,1)}), bf16[128,2,1024]{2,1,0:T(2,128)(2,1)}, u32[]{:S(2)}, u32[]{:S(2)}) async-start(bf16[128,2,1024]{2,1,0:T(2,128)(2,1)} %reshape.2548), calls=%async_computation.3 | async-start | bytes 1048576 | tf_op jit(solution)/shard_map/all_to_all | solution.py:115
  334.3 196.9 %all-reduce.8.cloned.1.call-start = ((), (), s32[]{:S(2)}) async-start(), calls=%async_computation.6 | async-start | bytes 655360 | tf_op jit(solution)/shard_map/psum | solution.py:180
  342.9 195.1 %copy-start.3 = (bf16[1440,1024]{0,1:T(8,128)(2,1)S(1)}, bf16[1440,1024]{0,1:T(8,128)(2,1)}, u32[]{:S(2)}) copy-start(bf16[1440,1024]{0,1:T(8,128)(2,1)} %copy-done.1) | copy-start | bytes 8847364
Sparse Core Ops, SparseCore 0:
  153.6 36.9 all-gather.2
  286.3 27.4 all-gather.4
  343.0 188.1 all-reduce.7
where the time goes:
time: 557 us; the launch traced here: 549 us
  waiting for transfers between devices  265 us (48%)
  local copies, waits for them, and re-layouts  84.6 us (15%)
  other arithmetic  80.3 us (14%)
  starting transfers between devices  48.9 us (9%)
  matrix products  28.3 us (5%)
  blocking collectives  26.7 us (5%)
  between operations  14.6 us (3%)
    psum x1, waiting for transfers between devices, body(): mix_total, gain_total = lax.psum((mix_part, gain_part), 'lat')  186 us
    while x496, other arithmetic  39.8 us
    all_gather x1, waiting for transfers between devices, body(): all_inputs = lax.all_gather(coeffs, 'ch', axis=2, tiled=True)  31.6 us
    all_to_all x2, starting transfers between devices, to_latitudes(): lax.all_to_all(values, 'lat', split_axis=2, concat_axis=2, tiled=True)  29.5 us
    unnamed x33, local copies, waits for them, and re-layouts  27.7 us
    all_gather x1, waiting for transfers between devices, body(): lax.all_gather(pre_grad, 'ch', axis=2, tiled=True)  27.5 us
    all_to_all x1, blocking collectives, to_orders(): lax.all_to_all(values, 'lat', split_axis=2, concat_axis=2, tiled=True)  26.7 us
    all_to_all x2, waiting for transfers between devices, to_latitudes(): lax.all_to_all(values, 'lat', split_axis=2, concat_axis=2, tiled=True)  19.9 us
  transfers between devices with their start and end apart: 6, of which 4 were waited for; matrix products, arithmetic and copies ran while one was open for 19% of the time, Pallas kernels for 0%

commit v1 on v0

v1 whole, which is shorter than its diff:
```python
import functools
import math

import jax
import jax.numpy as jnp
import numpy as np
from jax import lax
from jax.experimental import pallas as pl
from jax.experimental.pallas import tpu as pltpu
from jax.sharding import PartitionSpec as P

MESH = pl.DeviceIdType.MESH
BF, F32 = jnp.bfloat16, jnp.float32
CL, JL, NLON = 64, 4, 1440
NZ, NY, NC, NX = 8, 8, 2, 4
NLAT, MODES = 512, 512
RENEW = 32
VMEM_BYTES = 56 * 1024 * 1024
NN = (((1,), (0,)), ((), ()))
NT = (((1,), (1,)), ((), ()))
TN = (((0,), (0,)), ((), ()))


def dot(a, b, dims=NN):
    return lax.dot_general(a, b, dims, preferred_element_type=F32)


def half_angle(steps):
    turns = jnp.floor(steps * (1.0 / NLON) + 0.5)
    t = (steps - turns * NLON) * (math.pi / NLON)
    u = t * t
    s = t * (1.0 + u * (-1.0 / 6 + u * (1.0 / 120 + u * (-1.0 / 5040 + u * (1.0 / 362880 + u * (-1.0 / 39916800))))))
    c = 1.0 + u * (-0.5 + u * (1.0 / 24 + u * (-1.0 / 720 + u * (1.0 / 40320 + u * (-1.0 / 3628800 + u * (1.0 / 479001600))))))
    return 1.0 - 2.0 * s * s, 2.0 * s * c


def tables_kernel(slots_ref, logs_ref, mcol_ref, cosv_ref, logsin_ref, f_ref, l_ref, lt_ref, up_ref, low_ref, raw_ref):
    slot = lax.axis_index("lat") * NX + lax.axis_index("ch")
    order = slots_ref[slot]
    m = order.astype(F32)

    def long_rows(i, carry):
        rows = pl.ds(pl.multiple_of(i * 64, 64), 64)
        mc = jnp.broadcast_to(mcol_ref[rows, :].astype(F32), (64, 128))
        lane = lax.broadcasted_iota(jnp.int32, (64, 128), 1).astype(F32)
        cb, sb = half_angle(mc * lane)
        ca, sa = half_angle(mc * (lane * 128.0))
        cb, sb = cb * math.sqrt(2.0 / NLON), sb * math.sqrt(2.0 / NLON)
        for a in range(12):
            width = min(128, NLON - a * 128)
            cav = jnp.broadcast_to(ca[:, a : a + 1], (64, 128))
            sav = jnp.broadcast_to(sa[:, a : a + 1], (64, 128))
            f_ref[0, rows, a * 128 : a * 128 + width] = (cav * cb - sav * sb).astype(BF)[:, :width]
            f_ref[1, rows, a * 128 : a * 128 + width] = (-(sav * cb + cav * sb)).astype(BF)[:, :width]
        return carry

    lax.fori_loop(0, 8, long_rows, 0)

    k = lax.broadcasted_iota(jnp.int32, (MODES, 128), 0).astype(F32)
    degree = k + (m + 1.0)
    upper = jnp.sqrt((4.0 * degree * degree - 1.0) / (degree * degree - m * m))
    below = degree - 1.0
    lower = jnp.sqrt((below * below - m * m) / jnp.maximum(4.0 * below * below - 1.0, 1.0))
    up_ref[...] = upper
    low_ref[...] = upper * lower
    cosv = cosv_ref[...]
    start = 0.5 * (jnp.log(jnp.full((4, 128), m + 0.5, F32)) + logs_ref[order]) + m * logsin_ref[...]

    def block(b, carry):
        previous, current, scale = carry
        factor = jnp.exp(0.5 * scale)
        for offset in range(RENEW):
            step = b * RENEW + offset
            raw_ref[pl.ds(pl.multiple_of(step * 4, 4), 4), :] = current * factor * factor
            ua = jnp.broadcast_to(up_ref[pl.ds(step, 1), :], (4, 128)) * cosv
            lb = jnp.broadcast_to(low_ref[pl.ds(step, 1), :], (4, 128))
            previous, current = current, ua * current - lb * previous
        biggest = jnp.maximum(jnp.abs(previous), jnp.abs(current))
        shift = jnp.log(biggest)
        rescale = jnp.exp(-shift)
        return previous * rescale, current * rescale, scale + shift

    zero = jnp.zeros((4, 128), F32)
    lax.fori_loop(0, MODES // RENEW, block, (zero, zero + 1.0, start))
    live = lax.broadcasted_iota(jnp.int32, (MODES, 128), 0) < MODES - order
    for g in range(4):
        part = raw_ref[pl.ds(g, MODES, stride=4), :]
        part = jnp.where(live, part, 0.0) * math.sqrt(math.pi / NLAT)
        l_ref[:, g * 128 : (g + 1) * 128] = part.astype(BF)
        lt_ref[g * 128 : (g + 1) * 128, :] = jnp.transpose(part).astype(BF)


def tables(order_slots):
    theta = math.pi * (np.arange(NLAT) + 0.5) / NLAT
    cosv = jnp.asarray(np.cos(theta).reshape(4, 128), F32)
    logsin = jnp.asarray(np.log(np.sin(theta)).reshape(4, 128), F32)
    s = np.arange(1, MODES)
    logs = jnp.asarray(np.concatenate([[0.0], np.cumsum(np.log((2.0 * s - 1.0) / (2.0 * s)))]), F32)
    vm = pl.BlockSpec(memory_space=pltpu.VMEM)
    sm = pl.BlockSpec(memory_space=pltpu.SMEM)
    return pl.pallas_call(
        tables_kernel,
        out_shape=(
            jax.ShapeDtypeStruct((2, MODES, NLON), BF),
            jax.ShapeDtypeStruct((MODES, NLAT), BF),
            jax.ShapeDtypeStruct((NLAT, MODES), BF),
        ),
        in_specs=[sm, sm, vm, vm, vm],
        out_specs=(vm, vm, vm),
        scratch_shapes=[
            pltpu.VMEM((MODES, 128), F32),
            pltpu.VMEM((MODES, 128), F32),
            pltpu.VMEM((MODES * 4, 128), F32),
        ],
        compiler_params=pltpu.CompilerParams(vmem_limit_bytes=VMEM_BYTES),
        name="tables",
    )(order_slots, logs, order_slots.reshape(MODES, 1), cosv, logsin)


def pack_blocks(g0, g1, perm_ref, out_ref, stage_ref):
    for j in range(JL):
        cols = slice(j * CL, (j + 1) * CL)
        stage_ref[j] = jnp.concatenate([g0[:, cols], g1[:, cols]], axis=1).astype(BF)
    for g in range(4):
        rows = jnp.concatenate([stage_ref[j, g * 128 : (g + 1) * 128, :] for j in range(JL)], axis=0)
        out_ref[g * 32 : (g + 1) * 32] = dot(perm_ref[...], rows).astype(BF).reshape(32, 16, 128)


def unpack_blocks(r_ref, perm_ref, half, grid_ref):
    for g in range(4):
        rows = r_ref[g * 32 : (g + 1) * 32].reshape(512, 128)
        turned = dot(rows, perm_ref[...], TN)
        for j in range(JL):
            piece = turned[:, j * 128 : (j + 1) * 128]
            if half is not None:
                piece = piece * half[:, g * 128 : (g + 1) * 128]
            piece = piece.astype(BF)
            for r in range(2):
                grid_ref[r, j * CL : (j + 1) * CL, g * 128 : (g + 1) * 128] = piece[r * CL : (r + 1) * CL]


def first_kernel(x_ref, f_ref, sine_ref, perm_ref, out_ref, stage_ref):
    sines = sine_ref[...]
    g0 = dot(f_ref[0], x_ref[...], NT) * sines
    g1 = dot(f_ref[1], x_ref[...], NT) * sines
    pack_blocks(g0, g1, perm_ref, out_ref, stage_ref)


CHUNKS = ((0, 384), (384, 384), (768, 384), (1152, 288))


def middle_kernel(r_ref, x_ref, cot_ref, f_ref, halfrow_ref, halfcol_ref, perm_ref, y_ref, out_ref, grid_ref, slope_ref, stage_ref):
    unpack_blocks(r_ref, perm_ref, halfrow_ref[...], grid_ref)
    for first, width in CHUNKS:
        cols = slice(first, first + width)
        v = dot(grid_ref[0], f_ref[0, :, cols]) + dot(grid_ref[1], f_ref[1, :, cols])
        cdf = 0.5 * (1.0 + lax.erf(v * (1.0 / math.sqrt(2.0))))
        y_ref[:, cols] = (x_ref[:, cols].astype(F32) + v * cdf).astype(BF)
        slope = cdf + v * jnp.exp(-0.5 * v * v) * (1.0 / math.sqrt(2.0 * math.pi))
        slope_ref[:, cols] = (cot_ref[:, cols].astype(F32) * slope).astype(BF)
    hc = halfcol_ref[...]
    g0 = dot(f_ref[0], slope_ref[...], NT) * hc
    g1 = dot(f_ref[1], slope_ref[...], NT) * hc
    pack_blocks(g0, g1, perm_ref, out_ref, stage_ref)


def last_kernel(r_ref, cot_ref, f_ref, perm_ref, out_ref, grid_ref):
    unpack_blocks(r_ref, perm_ref, None, grid_ref)
    for first, width in CHUNKS:
        cols = slice(first, first + width)
        v = dot(grid_ref[0], f_ref[0, :, cols]) + dot(grid_ref[1], f_ref[1, :, cols])
        out_ref[:, cols] = (cot_ref[:, cols].astype(F32) + v).astype(BF)


def own_order(slots_ref):
    return slots_ref[lax.axis_index("lat") * NX + lax.axis_index("ch")]


def gain_rows(gain_ref, x, order):
    k = lax.broadcasted_iota(jnp.int32, (MODES, 128), 0)
    rolled = pltpu.roll(gain_ref[x], lax.rem(MODES - order, MODES), 0)
    return jnp.where(k < MODES - order, rolled, 0.0)


def forward_kernel(slots_ref, q_ref, l_ref, lt_ref, w_ref, gain_ref, coeff_ref, mixed_ref, spec_ref, ret_ref, flat_ref):
    order = own_order(slots_ref)
    values = jnp.concatenate([q_ref[x] for x in range(NX)], axis=1)
    coeff_ref[...] = dot(l_ref[...], values).astype(BF)
    mixed_ref[...] = dot(coeff_ref[...], w_ref[...]).astype(BF)
    for x in range(NX):
        cols = slice(x * 128, (x + 1) * 128)
        spec = mixed_ref[:, cols].astype(F32) * gain_rows(gain_ref, x, order)
        flat_ref[:, cols] = spec.astype(BF)
        spec_ref[x] = jnp.transpose(spec).astype(BF)
    ret = dot(lt_ref[...], flat_ref[...]).astype(BF)
    for x in range(NX):
        ret_ref[x] = ret[:, x * 128 : (x + 1) * 128]


def backward_kernel(slots_ref, q_ref, l_ref, lt_ref, w_ref, gain_ref, coeff_ref, mixed_ref, sine_ref, ret_ref, sums_ref, pre_ref):
    order = own_order(slots_ref)
    values = jnp.concatenate([q_ref[x] for x in range(NX)], axis=1)
    grad = dot(l_ref[...], values)
    for x in range(NX):
        cols = slice(x * 128, (x + 1) * 128)
        part = grad[:, cols]
        pre_ref[:, cols] = (part * gain_rows(gain_ref, x, order)).astype(BF)
        prod = pltpu.roll(part * mixed_ref[:, cols].astype(F32), order, 0)
        prod = prod[:, :CL] + prod[:, CL:]
        sums_ref[x, 128:384, :] = jnp.concatenate([prod[:256], prod[256:]], axis=1)
    mix = dot(coeff_ref[...], pre_ref[...], TN)
    for x in range(NX):
        blocks = []
        for i in range(NX):
            a = mix[i * 128 : i * 128 + CL, x * 128 : x * 128 + CL]
            b = mix[i * 128 + CL : (i + 1) * 128, x * 128 + CL : (x + 1) * 128]
            blocks.append(a + b)
        low = jnp.concatenate([blocks[0], blocks[1]], axis=0)
        high = jnp.concatenate([blocks[2], blocks[3]], axis=0)
        sums_ref[x, 0:128, :] = jnp.concatenate([low, high], axis=1)
    back = dot(pre_ref[...], w_ref[...], NT).astype(BF)
    ret = (dot(lt_ref[...], back) * sine_ref[...]).astype(BF)
    for x in range(NX):
        ret_ref[x] = ret[:, x * 128 : (x + 1) * 128]


class Place:
    def __init__(self):
        lat = lax.axis_index("lat")
        self.x = lax.axis_index("ch")
        self.c = lax.rem(lat, 2)
        self.y = lax.rem(lax.div(lat, 2), 8)
        self.z = lax.div(lat, 16)

    def at(self, z=None, y=None, c=None, x=None):
        z, y = (self.z if z is None else z), (self.y if y is None else y)
        c, x = (self.c if c is None else c), (self.x if x is None else x)
        return ((z * 8 + y) * 2 + c, x)


def around(value, step, count):
    return lax.rem(value + step, count)


def send(src, dst, ssem, rsem, target):
    pltpu.make_async_remote_copy(
        src_ref=src, dst_ref=dst, send_sem=ssem, recv_sem=rsem, device_id=target, device_id_type=MESH
    ).start()


def settle(view, sem):
    pltpu.make_async_copy(view, view, sem).wait()


def greet(me):
    barrier = pltpu.get_barrier_semaphore()
    other = 1 - me.c
    targets = [me.at(c=other)]
    for o in range(1, 8):
        targets += [me.at(y=around(me.y, o, 8)), me.at(z=around(me.z, o, 8))]
        targets += [me.at(y=around(me.y, o, 8), c=other), me.at(z=around(me.z, o, 8), c=other)]
    for o in range(1, 4):
        targets.append(me.at(x=around(me.x, o, 4)))
    for target in targets:
        pl.semaphore_signal(barrier, inc=1, device_id=target, device_id_type=MESH)
    pl.semaphore_wait(barrier, len(targets))


def lat_start(me, s_ref, ta_ref, tb_ref, ssem, rsem, lsem):
    pltpu.make_async_copy(s_ref.at[:, me.y, 0], ta_ref.at[me.y], lsem.at[0]).start()
    pltpu.make_async_copy(s_ref.at[me.z, :, 1], tb_ref.at[me.z], lsem.at[1]).start()
    for o in range(1, 8):
        y, z = around(me.y, o, 8), around(me.z, o, 8)
        send(s_ref.at[:, y, 0], ta_ref.at[me.y], ssem.at[0], rsem.at[0], me.at(y=y))
        send(s_ref.at[z, :, 1], tb_ref.at[me.z], ssem.at[1], rsem.at[1], me.at(z=z))


def lat_middle(me, ta_ref, tb_ref, r_ref, ssem, rsem, lsem):
    settle(ta_ref.at[0], lsem.at[0])
    settle(ta_ref.at[0:7], rsem.at[0])
    settle(tb_ref.at[0], lsem.at[1])
    settle(tb_ref.at[0:7], rsem.at[1])
    here_a, here_b = r_ref.at[me.z, :, me.c], r_ref.at[:, me.y, me.c]
    to_a, to_b = 2 + me.c, 3 - me.c
    for o in range(1, 8):
        y, z = around(me.y, o, 8), around(me.z, o, 8)
        send(ta_ref.at[:, z], here_a, ssem.at[to_a], rsem.at[to_a], me.at(z=z, c=0))
        send(tb_ref.at[:, y], here_b, ssem.at[to_b], rsem.at[to_b], me.at(y=y, c=1))

    @pl.when(me.c == 0)
    def _():
        pltpu.make_async_copy(ta_ref.at[:, me.z], here_a, lsem.at[2]).start()
        send(tb_ref.at[:, me.y], here_b, ssem.at[3], rsem.at[3], me.at(c=1))

    @pl.when(me.c == 1)
    def _():
        pltpu.make_async_copy(tb_ref.at[:, me.y], here_b, lsem.at[2]).start()
        send(ta_ref.at[:, me.z], here_a, ssem.at[3], rsem.at[3], me.at(c=0))


def lat_end(ta_ref, lsem, rsem):
    settle(ta_ref.at[0], lsem.at[2])
    settle(ta_ref.at[0:7], rsem.at[2])
    settle(ta_ref, rsem.at[3])


def lat_sent(ta_ref, ssem):
    settle(ta_ref.at[0:7], ssem.at[0])
    settle(ta_ref.at[0:7], ssem.at[1])
    settle(ta_ref.at[0:7], ssem.at[2])
    settle(ta_ref, ssem.at[3])


def x_start(me, src_ref, dst_ref, ssem, rsem, lsem):
    for o in (2, 1, 3):
        x = around(me.x, o, 4)
        send(src_ref.at[x], dst_ref.at[me.x], ssem, rsem, me.at(x=x))
    pltpu.make_async_copy(src_ref.at[me.x], dst_ref.at[me.x], lsem).start()


def x_end(dst_ref, rsem, lsem):
    settle(dst_ref.at[0], lsem)
    settle(dst_ref.at[0:3], rsem)


def to_orders_kernel(s_ref, perm_ref, q_ref, ta_ref, tb_ref, r_ref, p_ref, ssem, rsem, lsem):
    me = Place()
    greet(me)
    lat_start(me, s_ref, ta_ref, tb_ref, ssem, rsem, lsem)
    lat_middle(me, ta_ref, tb_ref, r_ref, ssem, rsem, lsem)
    lat_end(ta_ref, lsem, rsem)

    def turn(g, carry):
        rows = r_ref[g].reshape(256, 128)
        out = dot(perm_ref[...], rows).astype(BF)
        at = pl.ds(pl.multiple_of(g * 64, 64), 64)
        for s in range(4):
            p_ref[s, at, :] = out[s * 64 : (s + 1) * 64]
        return carry

    lax.fori_loop(0, 8, turn, 0)
    x_start(me, p_ref, q_ref, ssem.at[4], rsem.at[4], lsem.at[3])
    x_end(q_ref, rsem.at[4], lsem.at[3])
    lat_sent(ta_ref, ssem)
    settle(p_ref.at[0:3], ssem.at[4])


def spread(t_ref, perm_ref, s_ref):
    def turn(g, carry):
        at = pl.ds(pl.multiple_of(g * 64, 64), 64)
        rows = jnp.concatenate([t_ref[s, at, :] for s in range(4)], axis=0)
        s_ref[g] = dot(perm_ref[...], rows).astype(BF).reshape(8, 2, 16, 128)
        return carry

    lax.fori_loop(0, 8, turn, 0)


def to_grid_kernel(ret_ref, spec_ref, perm_ref, r_ref, out_ref, t_ref, s_ref, ta_ref, tb_ref, ssem, rsem, lsem):
    me = Place()
    greet(me)
    x_start(me, ret_ref, t_ref, ssem.at[4], rsem.at[4], lsem.at[3])
    x_start(me, spec_ref, out_ref, ssem.at[5], rsem.at[5], lsem.at[4])
    x_end(t_ref, rsem.at[4], lsem.at[3])
    spread(t_ref, perm_ref, s_ref)
    lat_start(me, s_ref, ta_ref, tb_ref, ssem, rsem, lsem)
    lat_middle(me, ta_ref, tb_ref, r_ref, ssem, rsem, lsem)
    lat_end(ta_ref, lsem, rsem)
    x_end(out_ref, rsem.at[5], lsem.at[4])
    lat_sent(ta_ref, ssem)
    settle(t_ref.at[0:3], ssem.at[4])
    settle(out_ref.at[0:3], ssem.at[5])


def to_grid_sums_kernel(
    ret_ref, sums_ref, perm_ref, r_ref, total_ref,
    t_ref, s_ref, ta_ref, tb_ref, v_ref, half_ref, core_ref, own_ref, ybuf_ref, piece_ref, zbuf_ref, fin_ref,
    ssem, rsem, lsem,
):
    me = Place()
    other = 1 - me.c
    greet(me)
    x_start(me, ret_ref, t_ref, ssem.at[4], rsem.at[4], lsem.at[3])
    x_start(me, sums_ref, v_ref, ssem.at[5], rsem.at[5], lsem.at[4])
    x_end(t_ref, rsem.at[4], lsem.at[3])
    spread(t_ref, perm_ref, s_ref)
    lat_start(me, s_ref, ta_ref, tb_ref, ssem, rsem, lsem)
    x_end(v_ref, rsem.at[5], lsem.at[4])
    half_ref[...] = ((v_ref[0] + v_ref[1]) + (v_ref[2] + v_ref[3])).reshape(2, 192, 128)
    send(half_ref.at[other], core_ref, ssem.at[6], rsem.at[6], me.at(c=other))
    lat_middle(me, ta_ref, tb_ref, r_ref, ssem, rsem, lsem)
    settle(core_ref, rsem.at[6])
    own_ref[...] = (half_ref[me.c] + core_ref[...]).reshape(8, 24, 128)
    for o in range(1, 8):
        y = around(me.y, o, 8)
        send(own_ref.at[y], ybuf_ref.at[me.y], ssem.at[7], rsem.at[7], me.at(y=y))
    ybuf_ref[me.y] = own_ref[me.y]
    settle(ybuf_ref.at[0:7], rsem.at[7])
    piece_ref[...] = jnp.sum(ybuf_ref[...], axis=0)
    for o in range(1, 8):
        z = around(me.z, o, 8)
        send(piece_ref, zbuf_ref.at[me.z], ssem.at[8], rsem.at[8], me.at(z=z))
    zbuf_ref[me.z] = piece_ref[...]
    settle(zbuf_ref.at[0:7], rsem.at[8])
    fin_ref[...] = jnp.sum(zbuf_ref[...], axis=0)
    for o in range(8):
        y = around(me.y, o, 8)
        if o > 0:
            send(fin_ref, total_ref.at[me.c, me.y], ssem.at[9], rsem.at[9], me.at(y=y))
        send(fin_ref, total_ref.at[me.c, me.y], ssem.at[10], rsem.at[10], me.at(y=y, c=other))
    total_ref[me.c, me.y] = fin_ref[...]
    lat_end(ta_ref, lsem, rsem)
    settle(total_ref.at[0, 0:7], rsem.at[9])
    settle(total_ref.at[0], rsem.at[10])
    lat_sent(ta_ref, ssem)
    settle(t_ref.at[0:3], ssem.at[4])
    settle(v_ref.at[0:3], ssem.at[5])
    settle(core_ref, ssem.at[6])
    settle(ybuf_ref.at[0:7], ssem.at[7])
    settle(zbuf_ref.at[0:7], ssem.at[8])
    settle(total_ref.at[0, 0:7], ssem.at[9])
    settle(total_ref.at[0], ssem.at[10])


VM = pl.BlockSpec(memory_space=pltpu.VMEM)
SM = pl.BlockSpec(memory_space=pltpu.SMEM)
BLOCKS = (NZ, NY, NC, 16, 128)


def local_call(kernel, outs, scratch, specs, name):
    return pl.pallas_call(
        kernel,
        out_shape=tuple(jax.ShapeDtypeStruct(*o) for o in outs),
        in_specs=specs,
        out_specs=tuple(VM for _ in outs),
        scratch_shapes=[pltpu.VMEM(*s) for s in scratch],
        compiler_params=pltpu.CompilerParams(vmem_limit_bytes=VMEM_BYTES),
        name=name,
    )


def exchange_call(kernel, outs, scratch, count, sems, ident, name):
    return pl.pallas_call(
        kernel,
        out_shape=tuple(jax.ShapeDtypeStruct(*o) for o in outs),
        in_specs=[VM] * count,
        out_specs=tuple(VM for _ in outs),
        scratch_shapes=[pltpu.VMEM(*s) for s in scratch]
        + [pltpu.SemaphoreType.DMA((sems,)), pltpu.SemaphoreType.DMA((sems,)), pltpu.SemaphoreType.DMA((5,))],
        compiler_params=pltpu.CompilerParams(vmem_limit_bytes=VMEM_BYTES, collective_id=ident, has_side_effects=True),
        name=name,
    )


def to_orders(blocks, perm, ident):
    (out,) = exchange_call(
        to_orders_kernel,
        [((NX, NLAT, 128), BF)],
        [((8, 8, 16, 128), BF), ((8, 8, 16, 128), BF), (BLOCKS, BF), ((4, 512, 128), BF)],
        2, 5, ident, "to_orders_%d" % ident,
    )(blocks.reshape(BLOCKS), perm)
    return out


def one_hot(rows):
    out = np.zeros((rows.size, rows.size), np.float32)
    out[np.arange(rows.size), rows] = 1.0
    return out


def body(grid_field, order_slots, mix_weight, degree_gain, cotangent):
    lat = lax.axis_index("lat")
    d, s, j = np.meshgrid(np.arange(32), np.arange(4), np.arange(4), indexing="ij")
    perm = jnp.asarray(one_hot((j * 128 + d * 4 + s).reshape(-1)), BF)
    s, e, j = np.meshgrid(np.arange(4), np.arange(16), np.arange(4), indexing="ij")
    turn = one_hot((e * 16 + s * 4 + j).reshape(-1))
    fore, back = jnp.asarray(turn, BF), jnp.asarray(turn.T, BF)
    sines = np.sin(math.pi * (np.arange(NLAT) + 0.5) / NLAT).astype(np.float32)
    band = lax.dynamic_slice_in_dim(jnp.asarray(sines), lat * JL, JL)
    band_row = jnp.repeat(band, CL).reshape(1, JL * CL)
    sine_col = jnp.asarray(sines).reshape(NLAT, 1)
    halving = jnp.where(order_slots == 0, 0.5, 1.0).astype(F32)
    x = jnp.transpose(grid_field, (1, 0, 2)).reshape(JL * CL, NLON)
    cot = jnp.transpose(cotangent, (1, 0, 2)).reshape(JL * CL, NLON)
    parts = mix_weight.reshape(NX, 1, CL, NX, 1, CL)
    same = jnp.asarray(np.eye(2).reshape(1, 2, 1, 1, 2, 1), BF)
    weights = (parts * same).reshape(512, 512)
    turned = jnp.transpose(degree_gain)
    gains = lax.all_gather(jnp.concatenate([turned, turned], axis=1), "ch", axis=0)

    f_tab, leg, leg_t = tables(order_slots)
    (blocks,) = local_call(
        first_kernel, [((128, 16, 128), BF)], [((4, 512, 128), BF)], [VM] * 4, "first"
    )(x, f_tab, band_row, perm)
    q = to_orders(blocks, fore, 0)
    coeffs, mixed, spec, ret = local_call(
        forward_kernel,
        [((512, 512), BF), ((512, 512), BF), ((4, 128, 512), BF), ((4, 512, 128), BF)],
        [((512, 512), BF)],
        [SM] + [VM] * 5,
        "forward",
    )(order_slots, q, leg, leg_t, weights, gains)
    received, spectrum = exchange_call(
        to_grid_kernel,
        [(BLOCKS, BF), ((4, 128, 512), BF)],
        [((4, 512, 128), BF), (BLOCKS, BF), ((8, 8, 16, 128), BF), ((8, 8, 16, 128), BF)],
        3, 6, 1, "to_grid_1",
    )(ret, spec, back)
    out, blocks = local_call(
        middle_kernel,
        [((256, NLON), BF), ((128, 16, 128), BF)],
        [((2, 256, 512), BF), ((256, NLON), BF), ((4, 512, 128), BF)],
        [VM] * 7,
        "middle",
    )(received.reshape(128, 16, 128), x, cot, f_tab, halving.reshape(1, 512), halving.reshape(512, 1), perm)
    q = to_orders(blocks, fore, 2)
    ret, sums = local_call(
        backward_kernel,
        [((4, 512, 128), BF), ((4, 384, 128), F32)],
        [((512, 512), BF)],
        [SM] + [VM] * 8,
        "backward",
    )(order_slots, q, leg, leg_t, weights, gains, coeffs, mixed, sine_col)
    received, total = exchange_call(
        to_grid_sums_kernel,
        [(BLOCKS, BF), ((2, 8, 24, 128), F32)],
        [
            ((4, 512, 128), BF), (BLOCKS, BF), ((8, 8, 16, 128), BF), ((8, 8, 16, 128), BF),
            ((4, 384, 128), F32), ((2, 192, 128), F32), ((192, 128), F32), ((8, 24, 128), F32),
            ((8, 24, 128), F32), ((24, 128), F32), ((8, 24, 128), F32), ((24, 128), F32),
        ],
        3, 11, 3, "to_grid_3",
    )(ret, sums, back)
    (grad,) = local_call(
        last_kernel, [((256, NLON), BF)], [((2, 256, 512), BF)], [VM] * 4, "last"
    )(received.reshape(128, 16, 128), cot, f_tab, perm)

    total = total.reshape(384, 128)
    mix = jnp.concatenate([total[:128, :CL], total[:128, CL:]], axis=0) / MODES
    gain = jnp.concatenate([total[128:, :CL], total[128:, CL:]], axis=0).T / math.sqrt(MODES)
    out = jnp.transpose(out.reshape(JL, CL, NLON), (1, 0, 2))
    grad = jnp.transpose(grad.reshape(JL, CL, NLON), (1, 0, 2))
    return out, spectrum.reshape(4, 2, CL, MODES), grad, mix, gain


def solution(mesh):
    placed = (P("ch", "lat", None), P(), P(), P("ch", None), P("ch", "lat", None))
    return jax.shard_map(
        body,
        mesh=mesh,
        in_specs=placed,
        out_specs=(
            P("ch", "lat", None),
            P("lat", None, "ch", None),
            P("ch", "lat", None),
            P(None, "ch"),
            P("ch", None),
        ),
        check_vma=False,
    )
```

time: 557 us -> 228 us (0.41); the launches traced: 549 us -> 227 us
  waiting for transfers between devices: 265 us -> 0.04 us
  Pallas kernels: 0 us -> 190 us
  other arithmetic: 80.3 us -> 5.38 us
  local copies, waits for them, and re-layouts: 84.6 us -> 17.7 us
  starting transfers between devices: 48.9 us -> 0.04 us
  matrix products: 28.3 us -> 0 us
  blocking collectives: 26.7 us -> 0 us
    pallas_call x0 -> x10, Pallas kernels: none -> 190 us  [the longest x2 69.7 us: to_orders(): exchange_call(to_orders_kernel, [((NX, NLAT, 128), BF)], [((8, 8, 16, 128...]
    psum x1 -> x0, waiting for transfers between devices: 186 us -> none  [body(): mix_total, gain_total = lax.psum((mix_part, gain_part), 'lat')]
    all_gather x2 -> x1, waiting for transfers between devices: 59.1 us -> 0.02 us  [body(): lax.all_gather(jnp.concatenate([turned, turned], axis=1), 'ch', axis=0)]
    all_to_all x3 -> x0, starting transfers between devices: 48.4 us -> none  [the longest x2 29.5 us: to_latitudes(): lax.all_to_all(values, 'lat', split_axis=2, concat_axis=2, tiled=True)]
    while x496 -> x0, other arithmetic: 39.8 us -> none
    dot_general x10 -> x0, matrix products: 28.3 us -> none  [the longest x1 4.39 us: body(): jnp.einsum('cjq,nq->cjn', grid_side, forward_tab, preferred_element_type=...]
    all_to_all x1 -> x0, blocking collectives: 26.7 us -> none  [to_orders(): lax.all_to_all(values, 'lat', split_axis=2, concat_axis=2, tiled=True)]
    unnamed x33 -> x15, local copies, waits for them, and re-layouts: 27.7 us -> 1.13 us
  transfers between devices with their start and end apart: 6 -> 1, of which waited for: 4 -> 0; matrix products, arithmetic and copies ran while one was open for 19% -> 5% of each run, Pallas kernels for 0% -> 23%
where the time goes in v1:
time: 228 us; the launch traced here: 227 us
  Pallas kernels  190 us (83%)
  local copies, waits for them, and re-layouts  17.7 us (8%)
  between operations  14.2 us (6%)
  other arithmetic  5.38 us (2%)
    pallas_call x2, Pallas kernels, to_orders(): exchange_call(to_orders_kernel, [((NX, NLAT, 128), BF)], [((8, 8, 16, 128...  69.7 us
    pallas_call x1, Pallas kernels, body(): exchange_call(to_grid_sums_kernel, [(BLOCKS, BF), ((2, 8, 24, 128), F32)]...  48.6 us
    pallas_call x1, Pallas kernels, body(): exchange_call(to_grid_kernel, [(BLOCKS, BF), ((4, 128, 512), BF)], [((4,...  36.7 us
    pallas_call x1, Pallas kernels, tables(): pl.pallas_call(tables_kernel, out_shape=(jax.ShapeDtypeStruct((2, MODES,...  8.02 us
    pallas_call x1, Pallas kernels, body(): local_call(middle_kernel, [((256, NLON), BF), ((128, 16, 128), BF)], [((2...  7.16 us
    pallas_call x1, Pallas kernels, body(): local_call(backward_kernel, [((4, 512, 128), BF), ((4, 384, 128), F32)],...  5.32 us
    pallas_call x1, Pallas kernels, body(): local_call(last_kernel, [((256, NLON), BF)], [((2, 256, 512), BF)], [VM]...  4.99 us
    pallas_call x1, Pallas kernels, body(): local_call(first_kernel, [((128, 16, 128), BF)], [((4, 512, 128), BF)], [...  4.81 us
  transfers between devices with their start and end apart: 1, of which 0 were waited for; matrix products, arithmetic and copies ran while one was open for 5% of the time, Pallas kernels for 23%

profile of v1, /device:TPU:1, one launch (start us, length us, event | category | flops | bytes accessed | tf_op | source)
XLA Modules:
  0.0 227.1 jit_solution(6159579158481284094)
XLA Ops:
  7.2 0.0 copy-start
  7.2 0.0 copy-start.1
  7.2 0.0 all-gather.3.cloned.1.call-start
  7.2 1.8 pad_maximum_fusion
  9.0 0.0 all-gather.3.cloned.1.call-update
  9.1 0.8 dynamic_slice.3
  9.8 0.1 broadcast_in_dim.11
  9.9 0.6 reshape_reshape.3.sine_ref
  10.5 0.7 compare_select_fusion
  11.2 0.0 copy-start.4
  11.2 0.9 copy.31.halfcol_ref
  12.1 1.1 mul.25
  13.2 1.5 copy.28.mcol_ref
  14.7 1.6 broadcast_multiply_fusion
  16.3 1.4 mul.30.w_ref
  17.7 0.0 copy-done
  17.7 1.0 copy.27
  18.7 0.0 copy-done.1
  18.7 1.0 copy.30
  19.8 0.0 copy-done.4
  19.8 8.0 %tables.1 = (bf16[2,512,1440]{2,1,0:T(8,128)(2,1)}, bf16[512,512]{1,0:T(8,128)(2,1)}, bf16[512,512]{1,0:T(8,128)(2,1)}) custom-call(s32[512]{0:T(512)} %slots_ref.5, f32[512]{0:T(512)} %constant.46.clone.logs_ref, s32[512,1]{1,0:T(8,128)} %copy.28.mcol_ref, f32[4,128]{1,0:T(4,128)} %constant.44.clone.cosv_ref, f32[4,128]{1,0:T(4,128)} %constant.45.clone.logsin_ref), custom_call_target="tpu_custom_call" | custom-call | tf_op jit(solution)/shard_map/tables/pallas_call | solution.py:101
  27.8 4.8 %first.1 = bf16[128,16,128]{2,1,0:T(8,128)(2,1)} custom-call(bf16[256,1440]{1,0:T(8,128)(2,1)} %bitcast.27, bf16[2,512,1440]{2,1,0:T(8,128)(2,1)} %get-tuple-element.20.f_ref, f32[1,256]{1,0:T(1,128)} %reshape_reshape.3.sine_ref, bf16[512,512]{1,0:T(8,128)(2,1)} %constant.39.clone.perm_ref), custom_call_target="tpu_custom_call" | custom-call | tf_op jit(solution)/shard_map/first/pallas_call | solution.py:491
  32.6 38.9 %to_orders_0.1.q_ref = bf16[4,512,128]{2,1,0:T(8,128)(2,1)} custom-call(bf16[8,8,2,16,128]{4,3,2,1,0:T(8,128)(2,1)} %bitcast.30, bf16[256,256]{1,0:T(8,128)(2,1)} %constant.40.clone.perm_ref), custom_call_target="tpu_custom_call" | custom-call | tf_op jit(solution)/shard_map/to_orders_0/pallas_call | solution.py:455
  71.5 0.0 all-gather.3.cloned.1.call-done
  71.5 2.6 %copy.29 = f32[2048,128]{1,0:T(8,128)} copy(f32[2048,128]{0,1:T(8,128)} %all-gather.3.cloned.1.call-done) | data formatting | bytes 2097152 | tf_op jit(solution)/shard_map/all_gather | solution.py:488
  74.1 4.4 %forward.1 = (bf16[512,512]{1,0:T(8,128)(2,1)}, bf16[512,512]{1,0:T(8,128)(2,1)}, bf16[4,128,512]{2,1,0:T(8,128)(2,1)}, bf16[4,512,128]{2,1,0:T(8,128)(2,1)}) custom-call(s32[512]{0:T(512)} %slots_ref.5, bf16[4,512,128]{2,1,0:T(8,128)(2,1)} %to_orders_0.1.q_ref, bf16[512,512]{1,0:T(8,128)(2,1)} %get-tuple-element.21.l_ref, ...), custom_call_target="tpu_custom_call" | custom-call | tf_op jit(solution)/shard_map/forward/pallas_call | solution.py:495
  78.6 36.7 %to_grid_1.1 = (bf16[8,8,2,16,128]{4,3,2,1,0:T(8,128)(2,1)}, bf16[4,128,512]{2,1,0:T(8,128)(2,1)}) custom-call(bf16[4,512,128]{2,1,0:T(8,128)(2,1)} %get-tuple-element.23.ret_ref, bf16[4,128,512]{2,1,0:T(8,128)(2,1)} %get-tuple-element.24.spec_ref, bf16[256,256]{1,0:T(8,128)(2,1)} %constant.41.clone.perm_ref), custom_call_target="tpu_custom_call" | custom-call | tf_op jit(solution)/shard_map/to_grid_1/pallas_call | solution.py:502
  115.3 7.2 %middle.1 = (bf16[256,1440]{1,0:T(8,128)(2,1)}, bf16[128,16,128]{2,1,0:T(8,128)(2,1)}) custom-call(bf16[128,16,128]{2,1,0:T(8,128)(2,1)} %bitcast.39, bf16[256,1440]{1,0:T(8,128)(2,1)} %bitcast.28, bf16[256,1440]{1,0:T(8,128)(2,1)} %bitcast.25, bf16[2,512,1440]{2,1,0:T(8,128)(2,1)} %get-tuple-element.20.f_ref, f32[1,512]{1,0:T(1,128)} %bitcast.43, ...), custom_call_target="tpu_custom_call" | custom-call | tf_op jit(solution)/shard_map/middle/pallas_call | solution.py:508
  122.5 30.8 %to_orders_2.1.q_ref = bf16[4,512,128]{2,1,0:T(8,128)(2,1)} custom-call(bf16[8,8,2,16,128]{4,3,2,1,0:T(8,128)(2,1)} %bitcast.37, bf16[256,256]{1,0:T(8,128)(2,1)} %constant.40.clone.perm_ref), custom_call_target="tpu_custom_call" | custom-call | tf_op jit(solution)/shard_map/to_orders_2/pallas_call | solution.py:455
  153.3 5.3 %backward.1 = (bf16[4,512,128]{2,1,0:T(8,128)(2,1)}, f32[4,384,128]{2,1,0:T(8,128)}) custom-call(s32[512]{0:T(512)} %slots_ref.5, bf16[4,512,128]{2,1,0:T(8,128)(2,1)} %to_orders_2.1.q_ref, bf16[512,512]{1,0:T(8,128)(2,1)} %get-tuple-element.21.l_ref, bf16[512,512]{1,0:T(8,128)(2,1)} %get-tuple-element.22.lt_ref, bf16[512,512]{1,0:T(8,128)(2,1)} %mul.30.w_ref, ...), custom_call_target="tpu_custom_call" | custom-call | tf_op jit(solution)/shard_map/backward/pallas_call | solution.py:516
  158.6 48.6 %to_grid_3.1 = (bf16[8,8,2,16,128]{4,3,2,1,0:T(8,128)(2,1)}, f32[2,8,24,128]{3,2,1,0:T(8,128)}) custom-call(bf16[4,512,128]{2,1,0:T(8,128)(2,1)} %get-tuple-element.31.ret_ref, f32[4,384,128]{2,1,0:T(8,128)} %get-tuple-element.32.sums_ref, bf16[256,256]{1,0:T(8,128)(2,1)} %constant.41.clone.perm_ref), custom_call_target="tpu_custom_call" | custom-call | tf_op jit(solution)/shard_map/to_grid_3/pallas_call | solution.py:523
  207.2 1.0 fusion.2
  208.2 1.1 fusion.1
  209.3 0.0 copy-start.2
  209.3 5.0 %last.1 = bf16[256,1440]{1,0:T(8,128)(2,1)} custom-call(bf16[128,16,128]{2,1,0:T(8,128)(2,1)} %bitcast.38, bf16[256,1440]{1,0:T(8,128)(2,1)} %bitcast.26, bf16[2,512,1440]{2,1,0:T(8,128)(2,1)} %get-tuple-element.20.f_ref, bf16[512,512]{1,0:T(8,128)(2,1)} %constant.39.clone.perm_ref), custom_call_target="tpu_custom_call" | custom-call | tf_op jit(solution)/shard_map/last/pallas_call | solution.py:533
  214.3 0.0 copy-start.3
  214.3 0.1 copy.38
  214.3 0.1 copy.39
  214.4 0.1 copy.40
  214.5 0.1 copy.41
  214.6 0.0 copy-done.2
  214.6 3.5 %copy_bitcast_fusion = (bf16[64,4,1440]{2,1,0:T(4,128)(2,1)}, bf16[64,4,1440]{2,1,0:T(4,128)(2,1)}) fusion(bf16[4,64,1440]{2,1,0:T(8,128)(2,1)} %bitcast.29, bf16[4,64,1440]{2,1,0:T(8,128)(2,1)S(1)} %bitcast.35), kind=kLoop, calls=%fused_computation | loop fusion | bytes 2949120 | tf_op jit(solution)/shard_map/transpose | solution.py:541
  218.1 0.6 maximum_multiply_fusion.1
  218.8 0.7 fusion
  219.4 0.0 copy-done.3
  219.4 0.8 copy.45
Async XLA Ops:
  7.2 10.6 %copy-start = (bf16[64,4,1440]{2,1,0:T(4,128)(2,1)S(1)}, bf16[64,4,1440]{2,1,0:T(4,128)(2,1)}, u32[]{:S(2)}) copy-start(bf16[64,4,1440]{2,1,0:T(4,128)(2,1)} %param.13) | copy-start | bytes 2211844
  7.2 11.6 %copy-start.1 = (bf16[64,4,1440]{2,1,0:T(4,128)(2,1)S(1)}, bf16[64,4,1440]{2,1,0:T(4,128)(2,1)}, u32[]{:S(2)}) copy-start(bf16[64,4,1440]{2,1,0:T(4,128)(2,1)} %param.17) | copy-start | bytes 2211844
  7.2 64.3 %all-gather.3.cloned.1.call-start = ((), (), s32[]{:S(2)}) async-start(), calls=%async_computation | async-start | bytes 1310720 | tf_op jit(solution)/shard_map/all_gather | solution.py:488
  11.2 8.5 %copy-start.4 = (f32[512]{0:T(512)}, f32[512]{0:T(512)S(1)}, u32[]{:S(2)}) copy-start(f32[512]{0:T(512)S(1)} %compare_select_fusion) | copy-start | bytes 6148
  209.3 5.3 %copy-start.2 = (bf16[256,1440]{1,0:T(8,128)(2,1)S(1)}, bf16[256,1440]{1,0:T(8,128)(2,1)}, u32[]{:S(2)}) copy-start(bf16[256,1440]{1,0:T(8,128)(2,1)} %get-tuple-element.26) | copy-start | bytes 2211844
  214.3 5.1 %copy-start.3 = (bf16[4,128,512]{2,1,0:T(8,128)(2,1)S(1)}, bf16[4,128,512]{2,1,0:T(8,128)(2,1)}, u32[]{:S(2)}) copy-start(bf16[4,128,512]{2,1,0:T(8,128)(2,1)} %get-tuple-element.27) | copy-start | bytes 1572868
Sparse Core Ops, SparseCore 0:
  10.1 33.8 all-gather.2

commit v2 on v1

v2 whole, which is shorter than its diff:
```python
import math

import jax
import jax.numpy as jnp
import numpy as np
from jax import lax
from jax.experimental import pallas as pl
from jax.experimental.pallas import tpu as pltpu
from jax.sharding import PartitionSpec as P

MESH = pl.DeviceIdType.MESH
BF, F32 = jnp.bfloat16, jnp.float32
CL, JL, NLON = 64, 4, 1440
NZ, NY, NC, NX = 8, 8, 2, 4
NLAT, MODES = 512, 512
RENEW = 32
VMEM_BYTES = 56 * 1024 * 1024
NN = (((1,), (0,)), ((), ()))
NT = (((1,), (1,)), ((), ()))
TN = (((0,), (0,)), ((), ()))


def dot(a, b, dims=NN):
    return lax.dot_general(a, b, dims, preferred_element_type=F32)


def half_angle(steps):
    turns = jnp.floor(steps * (1.0 / NLON) + 0.5)
    t = (steps - turns * NLON) * (math.pi / NLON)
    u = t * t
    s = t * (1.0 + u * (-1.0 / 6 + u * (1.0 / 120 + u * (-1.0 / 5040 + u * (1.0 / 362880 + u * (-1.0 / 39916800))))))
    c = 1.0 + u * (-0.5 + u * (1.0 / 24 + u * (-1.0 / 720 + u * (1.0 / 40320 + u * (-1.0 / 3628800 + u * (1.0 / 479001600))))))
    return 1.0 - 2.0 * s * s, 2.0 * s * c


def long_tables(mcol_ref, f_ref):
    def long_rows(i, carry):
        rows = pl.ds(pl.multiple_of(i * 64, 64), 64)
        mc = mcol_ref[rows, :]
        lane = lax.broadcasted_iota(jnp.int32, (64, 128), 1).astype(F32)
        cb, sb = half_angle(mc * lane)
        ca, sa = half_angle(mc * (lane * 128.0))
        cb, sb = cb * math.sqrt(2.0 / NLON), sb * math.sqrt(2.0 / NLON)
        for a in range(12):
            width = min(128, NLON - a * 128)
            cav = jnp.broadcast_to(ca[:, a : a + 1], (64, 128))
            sav = jnp.broadcast_to(sa[:, a : a + 1], (64, 128))
            f_ref[0, rows, a * 128 : a * 128 + width] = (cav * cb - sav * sb).astype(BF)[:, :width]
            f_ref[1, rows, a * 128 : a * 128 + width] = (-(sav * cb + cav * sb)).astype(BF)[:, :width]
        return carry

    lax.fori_loop(0, 8, long_rows, 0)


def legendre_start(m, logs, logsin_ref, up_ref, low_ref):
    k = lax.broadcasted_iota(jnp.int32, (MODES, 128), 0).astype(F32)
    degree = k + (m + 1.0)
    upper = jnp.sqrt((4.0 * degree * degree - 1.0) / (degree * degree - m * m))
    below = degree - 1.0
    lower = jnp.sqrt((below * below - m * m) / jnp.maximum(4.0 * below * below - 1.0, 1.0))
    up_ref[...] = upper
    low_ref[...] = upper * lower
    start = 0.5 * (jnp.log(jnp.full((4, 128), m + 0.5, F32)) + logs) + m * logsin_ref[...]
    zero = jnp.zeros((4, 128), F32)
    return zero, zero + 1.0, start


def legendre_steps(first, last, carry, cosv, up_ref, low_ref, raw_ref):
    def block(b, carry):
        previous, current, scale = carry
        factor = jnp.exp(0.5 * scale)
        for offset in range(RENEW):
            step = b * RENEW + offset
            raw_ref[pl.ds(pl.multiple_of(step * 4, 4), 4), :] = current * factor * factor
            ua = jnp.broadcast_to(up_ref[pl.ds(step, 1), :], (4, 128)) * cosv
            lb = jnp.broadcast_to(low_ref[pl.ds(step, 1), :], (4, 128))
            previous, current = current, ua * current - lb * previous
        biggest = jnp.maximum(jnp.abs(previous), jnp.abs(current))
        shift = jnp.log(biggest)
        rescale = jnp.exp(-shift)
        return previous * rescale, current * rescale, scale + shift

    return lax.fori_loop(first, last, block, carry)


def legendre_end(order, raw_ref, l_ref, lt_ref, shift_ref):
    live = lax.broadcasted_iota(jnp.int32, (MODES, 128), 0) < MODES - order
    for g in range(4):
        part = raw_ref[pl.ds(g, MODES, stride=4), :]
        part = jnp.where(live, part, 0.0) * math.sqrt(math.pi / NLAT)
        l_ref[:, g * 128 : (g + 1) * 128] = part.astype(BF)
        lt_ref[g * 128 : (g + 1) * 128, :] = jnp.transpose(part).astype(BF)
    k = lax.broadcasted_iota(jnp.int32, (MODES, MODES), 0)
    l = lax.broadcasted_iota(jnp.int32, (MODES, MODES), 1)
    shift_ref[...] = jnp.where(l - k == order, 1.0, 0.0).astype(BF)


def pack_blocks(g0, g1, perm_ref, s_ref, stage_ref):
    for j in range(JL):
        cols = slice(j * CL, (j + 1) * CL)
        stage_ref[j] = jnp.concatenate([g0[:, cols], g1[:, cols]], axis=1).astype(BF)
    for g in range(4):
        rows = jnp.concatenate([stage_ref[j, g * 128 : (g + 1) * 128, :] for j in range(JL)], axis=0)
        s_ref[2 * g : 2 * g + 2] = dot(perm_ref[...], rows).astype(BF).reshape(2, 8, 2, 16, 128)


def unpack_blocks(r_ref, perm_ref, half, grid_ref):
    for g in range(4):
        rows = r_ref[2 * g : 2 * g + 2].reshape(512, 128)
        turned = dot(rows, perm_ref[...], TN)
        for j in range(JL):
            piece = turned[:, j * 128 : (j + 1) * 128]
            if half is not None:
                piece = piece * half[:, g * 128 : (g + 1) * 128]
            piece = piece.astype(BF)
            for r in range(2):
                grid_ref[r, j * CL : (j + 1) * CL, g * 128 : (g + 1) * 128] = piece[r * CL : (r + 1) * CL]


CHUNKS = ((0, 384), (384, 384), (768, 384), (1152, 288))


def middle(grid_ref, x_ref, cot_ref, f_ref, y_ref, slope_ref):
    for first, width in CHUNKS:
        cols = slice(first, first + width)
        v = dot(grid_ref[0], f_ref[0, :, cols]) + dot(grid_ref[1], f_ref[1, :, cols])
        cdf = 0.5 * (1.0 + lax.erf(v * (1.0 / math.sqrt(2.0))))
        y_ref[:, cols] = (x_ref[:, cols].astype(F32) + v * cdf).astype(BF)
        slope = cdf + v * jnp.exp(-0.5 * v * v) * (1.0 / math.sqrt(2.0 * math.pi))
        slope_ref[:, cols] = (cot_ref[:, cols].astype(F32) * slope).astype(BF)


def last(grid_ref, cot_ref, f_ref, out_ref):
    for first, width in CHUNKS:
        cols = slice(first, first + width)
        v = dot(grid_ref[0], f_ref[0, :, cols]) + dot(grid_ref[1], f_ref[1, :, cols])
        out_ref[:, cols] = (cot_ref[:, cols].astype(F32) + v).astype(BF)


def mixing_weights(w_ref, w2_ref):
    zero = jnp.zeros((CL, CL), F32)
    for x in range(NX):
        slab = w_ref[x * CL : (x + 1) * CL, :].astype(F32)
        pieces = [slab[:, i * CL : (i + 1) * CL] for i in range(NX)]
        top = jnp.concatenate([a for p in pieces for a in (p, zero)], axis=1)
        low = jnp.concatenate([a for p in pieces for a in (zero, p)], axis=1)
        w2_ref[x * 128 : x * 128 + CL, :] = top.astype(BF)
        w2_ref[x * 128 + CL : (x + 1) * 128, :] = low.astype(BF)


def split_gain(gain_ref, out_ref):
    turned = jnp.transpose(gain_ref[...])
    high = turned.astype(BF).astype(F32)
    out_ref[...] = jnp.concatenate([high, turned - high], axis=1).astype(BF)


def gain_rows(shift_ref, garr_ref, rows_ref):
    for x in range(NX):
        both = dot(shift_ref[...], garr_ref[x])
        row = both[:, :CL] + both[:, CL:]
        rows_ref[:, x * 128 : (x + 1) * 128] = jnp.concatenate([row, row], axis=1)


def gain_sums(grad_ref, mixed_ref, shift_ref, sums_ref):
    for x in range(NX):
        cols = slice(x * 128, (x + 1) * 128)
        prod = grad_ref[:, cols] * mixed_ref[:, cols].astype(F32)
        prod = prod[:, :CL] + prod[:, CL:]
        high = prod.astype(BF).astype(F32)
        both = dot(shift_ref[...], jnp.concatenate([high, prod - high], axis=1).astype(BF), TN)
        both = both[:, :CL] + both[:, CL:]
        sums_ref[x, 128:384, :] = jnp.concatenate([both[:256], both[256:]], axis=1)


def mix_sums(coeff_ref, pre_ref, sums_ref):
    mix = dot(coeff_ref[...], pre_ref[...], TN)
    for x in range(NX):
        blocks = []
        for i in range(NX):
            a = mix[i * 128 : i * 128 + CL, x * 128 : x * 128 + CL]
            b = mix[i * 128 + CL : (i + 1) * 128, x * 128 + CL : (x + 1) * 128]
            blocks.append(a + b)
        low = jnp.concatenate([blocks[0], blocks[1]], axis=0)
        high = jnp.concatenate([blocks[2], blocks[3]], axis=0)
        sums_ref[x, 0:128, :] = jnp.concatenate([low, high], axis=1)


def flat(q_ref):
    return jnp.concatenate([q_ref[x] for x in range(NX)], axis=1)


def split_lanes(value, ref):
    for x in range(NX):
        ref[x] = value[:, x * 128 : (x + 1) * 128]


class Place:
    def __init__(self):
        lat = lax.axis_index("lat")
        self.x = lax.axis_index("ch")
        self.c = lax.rem(lat, 2)
        self.y = lax.rem(lax.div(lat, 2), 8)
        self.z = lax.div(lat, 16)

    def at(self, z=None, y=None, c=None, x=None):
        z, y = (self.z if z is None else z), (self.y if y is None else y)
        c, x = (self.c if c is None else c), (self.x if x is None else x)
        return ((z * 8 + y) * 2 + c, x)


def around(value, step, count):
    return lax.rem(value + step, count)


def send(src, dst, ssem, rsem, target):
    pltpu.make_async_remote_copy(
        src_ref=src, dst_ref=dst, send_sem=ssem, recv_sem=rsem, device_id=target, device_id_type=MESH
    ).start()


def settle(view, sem):
    pltpu.make_async_copy(view, view, sem).wait()


def greet(me):
    barrier = pltpu.get_barrier_semaphore()
    other = 1 - me.c
    targets = [me.at(c=other)]
    for o in range(1, 8):
        targets += [me.at(y=around(me.y, o, 8)), me.at(z=around(me.z, o, 8))]
        targets += [me.at(y=around(me.y, o, 8), c=other), me.at(z=around(me.z, o, 8), c=other)]
    for o in range(1, 4):
        targets.append(me.at(x=around(me.x, o, 4)))
    for target in targets:
        pl.semaphore_signal(barrier, inc=1, device_id=target, device_id_type=MESH)
    return len(targets)


def lat_start(me, s_ref, ta_ref, tb_ref, ssem, rsem, lsem):
    pltpu.make_async_copy(s_ref.at[:, me.y, 0], ta_ref.at[me.y], lsem.at[0]).start()
    pltpu.make_async_copy(s_ref.at[me.z, :, 1], tb_ref.at[me.z], lsem.at[1]).start()
    for o in range(1, 8):
        y, z = around(me.y, o, 8), around(me.z, o, 8)
        send(s_ref.at[:, y, 0], ta_ref.at[me.y], ssem.at[0], rsem.at[0], me.at(y=y))
        send(s_ref.at[z, :, 1], tb_ref.at[me.z], ssem.at[1], rsem.at[1], me.at(z=z))


def lat_middle(me, ta_ref, tb_ref, r_ref, ssem, rsem, lsem):
    settle(ta_ref.at[0], lsem.at[0])
    settle(ta_ref.at[0:7], rsem.at[0])
    settle(tb_ref.at[0], lsem.at[1])
    settle(tb_ref.at[0:7], rsem.at[1])
    here_a, here_b = r_ref.at[me.z, :, me.c], r_ref.at[:, me.y, me.c]
    to_a, to_b = 2 + me.c, 3 - me.c
    for o in range(1, 8):
        y, z = around(me.y, o, 8), around(me.z, o, 8)
        send(ta_ref.at[:, z], here_a, ssem.at[to_a], rsem.at[to_a], me.at(z=z, c=0))
        send(tb_ref.at[:, y], here_b, ssem.at[to_b], rsem.at[to_b], me.at(y=y, c=1))

    @pl.when(me.c == 0)
    def _():
        pltpu.make_async_copy(ta_ref.at[:, me.z], here_a, lsem.at[2]).start()
        send(tb_ref.at[:, me.y], here_b, ssem.at[3], rsem.at[3], me.at(c=1))

    @pl.when(me.c == 1)
    def _():
        pltpu.make_async_copy(tb_ref.at[:, me.y], here_b, lsem.at[2]).start()
        send(ta_ref.at[:, me.z], here_a, ssem.at[3], rsem.at[3], me.at(c=0))


def lat_end(ta_ref, lsem, rsem):
    settle(ta_ref.at[0], lsem.at[2])
    settle(ta_ref.at[0:7], rsem.at[2])
    settle(ta_ref, rsem.at[3])


def lat_sent(ta_ref, ssem):
    settle(ta_ref.at[0:7], ssem.at[0])
    settle(ta_ref.at[0:7], ssem.at[1])
    settle(ta_ref.at[0:7], ssem.at[2])
    settle(ta_ref, ssem.at[3])


def x_start(me, src_ref, dst_ref, ssem, rsem, lsem):
    for o in (2, 1, 3):
        x = around(me.x, o, 4)
        send(src_ref.at[x], dst_ref.at[me.x], ssem, rsem, me.at(x=x))
    pltpu.make_async_copy(src_ref.at[me.x], dst_ref.at[me.x], lsem).start()


def x_end(dst_ref, rsem, lsem):
    settle(dst_ref.at[0], lsem)
    settle(dst_ref.at[0:3], rsem)


def turn_blocks(r_ref, perm_ref, p_ref):
    def turn(g, carry):
        rows = r_ref[g].reshape(256, 128)
        out = dot(perm_ref[...], rows).astype(BF)
        at = pl.ds(pl.multiple_of(g * 64, 64), 64)
        for s in range(4):
            p_ref[s, at, :] = out[s * 64 : (s + 1) * 64]
        return carry

    lax.fori_loop(0, 8, turn, 0)


def spread(t_ref, perm_ref, s_ref):
    def turn(g, carry):
        at = pl.ds(pl.multiple_of(g * 64, 64), 64)
        rows = jnp.concatenate([t_ref[s, at, :] for s in range(4)], axis=0)
        s_ref[g] = dot(perm_ref[...], rows, TN).astype(BF).reshape(8, 2, 16, 128)
        return carry

    lax.fori_loop(0, 8, turn, 0)


def whole_kernel(
    slots_ref, logs_ref, mrow_ref, cosv_ref, logsin_ref, band_ref, sine_ref, perm_ref, turn_ref, w_ref, gain_ref, x_ref, cot_ref,
    y_ref, spectrum_ref, out_ref, mix_ref, ggain_ref,
    f_ref, mcol_ref, up_ref, low_ref, raw_ref, l_ref, lt_ref, shift_ref, w2_ref, gsend_ref, garr_ref, grows_ref,
    stage_ref, grid_ref, slope_ref, coeff_ref, mixed_ref, flat_ref, pre_ref, grad_ref, spec_ref, ret_ref, ret2_ref,
    s_refs, ta_refs, tb_refs, r_refs, p_refs, q_refs,
    sums_ref, v_ref, half_ref, core_ref, own_ref, ybuf_ref, piece_ref, zbuf_ref, fin_ref, total_ref,
    ssem, rsem, lsem, xs, xr, xl, gs, gr,
):
    me = Place()
    other = 1 - me.c
    peers = greet(me)
    lat = lax.axis_index("lat")
    order = slots_ref[lat * NX + me.x]
    m = order.astype(F32)
    mrow = mrow_ref[...]
    half_row = jnp.where(mrow == 0, 0.5, 1.0)
    mcol_ref[...] = jnp.transpose(jnp.broadcast_to(mrow.astype(F32), (128, MODES)))
    split_gain(gain_ref, gsend_ref)
    long_tables(mcol_ref, f_ref)

    sines = band_ref[pl.ds(lat, 1), :]
    g0 = dot(f_ref[0], x_ref[...], NT) * sines
    g1 = dot(f_ref[1], x_ref[...], NT) * sines
    pack_blocks(g0, g1, perm_ref, s_refs.at[0], stage_ref)
    pl.semaphore_wait(pltpu.get_barrier_semaphore(), peers)

    def links(i):
        return ssem.at[i], rsem.at[i], lsem.at[i]

    def xlinks(i):
        return xs.at[i], xr.at[i], xl.at[i]

    def begin(i):
        lat_start(me, s_refs.at[i], ta_refs.at[i], tb_refs.at[i], *links(i))

    def carry_on(i):
        lat_middle(me, ta_refs.at[i], tb_refs.at[i], r_refs.at[i], *links(i))

    def finish(i):
        lat_end(ta_refs.at[i], lsem.at[i], rsem.at[i])

    begin(0)
    for o in range(1, 4):
        x = around(me.x, o, 4)
        send(gsend_ref, garr_ref.at[me.x], xs.at[6], xr.at[6], me.at(x=x))
    garr_ref[me.x] = gsend_ref[...]
    mixing_weights(w_ref, w2_ref)
    carry = legendre_start(m, logs_ref[order], logsin_ref, up_ref, low_ref)
    cosv = cosv_ref[...]
    carry = legendre_steps(0, 6, carry, cosv, up_ref, low_ref, raw_ref)
    carry_on(0)
    legendre_steps(6, MODES // RENEW, carry, cosv, up_ref, low_ref, raw_ref)
    legendre_end(order, raw_ref, l_ref, lt_ref, shift_ref)
    finish(0)
    turn_blocks(r_refs.at[0], turn_ref, p_refs.at[0])
    x_start(me, p_refs.at[0], q_refs.at[0], *xlinks(0))
    settle(garr_ref.at[0:3], xr.at[6])
    gain_rows(shift_ref, garr_ref, grows_ref)
    x_end(q_refs.at[0], xr.at[0], xl.at[0])

    coeff_ref[...] = dot(l_ref[...], flat(q_refs.at[0])).astype(BF)
    mixed_ref[...] = dot(coeff_ref[...], w2_ref[...]).astype(BF)
    flat_ref[...] = (mixed_ref[...].astype(F32) * grows_ref[...]).astype(BF)
    split_lanes(dot(lt_ref[...], flat_ref[...]).astype(BF), ret_ref)
    x_start(me, ret_ref, p_refs.at[1], *xlinks(1))
    for x in range(NX):
        spec_ref[x] = jnp.transpose(flat_ref[:, x * 128 : (x + 1) * 128].astype(F32)).astype(BF)
    x_start(me, spec_ref, spectrum_ref, *xlinks(2))
    x_end(p_refs.at[1], xr.at[1], xl.at[1])
    spread(p_refs.at[1], turn_ref, s_refs.at[1])
    begin(1)
    carry_on(1)
    finish(1)

    unpack_blocks(r_refs.at[1], perm_ref, half_row, grid_ref)
    middle(grid_ref, x_ref, cot_ref, f_ref, y_ref, slope_ref)
    mcol = mcol_ref[...]
    half_col = jnp.where(jnp.concatenate([mcol, mcol], axis=1) == 0.0, 0.5, 1.0)
    g0 = dot(f_ref[0], slope_ref[...], NT) * half_col
    g1 = dot(f_ref[1], slope_ref[...], NT) * half_col
    pack_blocks(g0, g1, perm_ref, s_refs.at[2], stage_ref)
    begin(2)
    carry_on(2)
    finish(2)
    turn_blocks(r_refs.at[2], turn_ref, p_refs.at[2])
    x_start(me, p_refs.at[2], q_refs.at[1], *xlinks(3))
    x_end(q_refs.at[1], xr.at[3], xl.at[3])

    grad_ref[...] = dot(l_ref[...], flat(q_refs.at[1]))
    pre_ref[...] = (grad_ref[...] * grows_ref[...]).astype(BF)
    back = dot(pre_ref[...], w2_ref[...], NT).astype(BF)
    split_lanes((dot(lt_ref[...], back) * sine_ref[...]).astype(BF), ret2_ref)
    x_start(me, ret2_ref, p_refs.at[3], *xlinks(4))
    gain_sums(grad_ref, mixed_ref, shift_ref, sums_ref)
    mix_sums(coeff_ref, pre_ref, sums_ref)
    x_start(me, sums_ref, v_ref, *xlinks(5))
    x_end(p_refs.at[3], xr.at[4], xl.at[4])
    spread(p_refs.at[3], turn_ref, s_refs.at[3])
    begin(3)
    x_end(v_ref, xr.at[5], xl.at[5])
    half_ref[...] = ((v_ref[0] + v_ref[1]) + (v_ref[2] + v_ref[3])).reshape(2, 192, 128)
    send(half_ref.at[other], core_ref, gs.at[0], gr.at[0], me.at(c=other))
    carry_on(3)
    settle(core_ref, gr.at[0])
    own_ref[...] = (half_ref[me.c] + core_ref[...]).reshape(8, 24, 128)
    for o in range(1, 8):
        y = around(me.y, o, 8)
        send(own_ref.at[y], ybuf_ref.at[me.y], gs.at[1], gr.at[1], me.at(y=y))
    ybuf_ref[me.y] = own_ref[me.y]
    settle(ybuf_ref.at[0:7], gr.at[1])
    piece_ref[...] = jnp.sum(ybuf_ref[...], axis=0)
    for o in range(1, 8):
        z = around(me.z, o, 8)
        send(piece_ref, zbuf_ref.at[me.z], gs.at[2], gr.at[2], me.at(z=z))
    zbuf_ref[me.z] = piece_ref[...]
    settle(zbuf_ref.at[0:7], gr.at[2])
    fin_ref[...] = jnp.sum(zbuf_ref[...], axis=0)
    for o in range(8):
        y = around(me.y, o, 8)
        if o > 0:
            send(fin_ref, total_ref.at[me.c, me.y], gs.at[3], gr.at[3], me.at(y=y))
        send(fin_ref, total_ref.at[me.c, me.y], gs.at[4], gr.at[4], me.at(y=y, c=other))
    total_ref[me.c, me.y] = fin_ref[...]
    finish(3)

    unpack_blocks(r_refs.at[3], perm_ref, None, grid_ref)
    last(grid_ref, cot_ref, f_ref, out_ref)
    settle(total_ref.at[0, 0:7], gr.at[3])
    settle(total_ref.at[0], gr.at[4])
    mix = total_ref[0].reshape(192, 128)[0:128] * (1.0 / MODES)
    mix_ref[...] = jnp.concatenate([mix[:, :CL], mix[:, CL:]], axis=0)
    gain = jnp.concatenate([total_ref[0].reshape(192, 128)[128:192], total_ref[1].reshape(192, 128)], axis=0)
    gain = jnp.concatenate([gain[:, :CL], gain[:, CL:]], axis=0) * (1.0 / math.sqrt(MODES))
    ggain_ref[...] = jnp.transpose(gain)

    for i in range(4):
        lat_sent(ta_refs.at[i], ssem.at[i])
    x_end(spectrum_ref, xr.at[2], xl.at[2])
    for i in range(5):
        settle(p_refs.at[0, 0:3], xs.at[i])
    settle(v_ref.at[0:3], xs.at[5])
    settle(garr_ref.at[0:3], xs.at[6])
    settle(core_ref, gs.at[0])
    settle(ybuf_ref.at[0:7], gs.at[1])
    settle(zbuf_ref.at[0:7], gs.at[2])
    settle(total_ref.at[0, 0:7], gs.at[3])
    settle(total_ref.at[0], gs.at[4])


VM = pl.BlockSpec(memory_space=pltpu.VMEM)
SM = pl.BlockSpec(memory_space=pltpu.SMEM)


def whole(*operands):
    scratch = [
        ((2, MODES, NLON), BF), ((MODES, 128), F32), ((MODES, 128), F32), ((MODES, 128), F32), ((MODES * 4, 128), F32),
        ((512, 512), BF), ((512, 512), BF), ((512, 512), BF), ((512, 512), BF), ((512, 128), BF), ((4, 512, 128), BF),
        ((512, 512), F32),
        ((4, 512, 128), BF), ((2, 256, 512), BF), ((256, NLON), BF), ((512, 512), BF), ((512, 512), BF), ((512, 512), BF),
        ((512, 512), BF), ((512, 512), F32), ((4, 128, 512), BF), ((4, 512, 128), BF), ((4, 512, 128), BF),
        ((4, NZ, NY, NC, 16, 128), BF), ((4, 8, 8, 16, 128), BF), ((4, 8, 8, 16, 128), BF), ((4, NZ, NY, NC, 16, 128), BF),
        ((4, 4, 512, 128), BF), ((2, 4, 512, 128), BF),
        ((4, 384, 128), F32), ((4, 384, 128), F32), ((2, 192, 128), F32), ((192, 128), F32), ((8, 24, 128), F32),
        ((8, 24, 128), F32), ((24, 128), F32), ((8, 24, 128), F32), ((24, 128), F32), ((2, 8, 24, 128), F32),
    ]
    sems = [(4, 4), (4, 4), (4, 3), (7,), (7,), (7,), (5,), (5,)]
    outs = [((256, NLON), BF), ((4, 128, 512), BF), ((256, NLON), BF), ((256, 64), F32), ((64, 512), F32)]
    return pl.pallas_call(
        whole_kernel,
        out_shape=tuple(jax.ShapeDtypeStruct(*o) for o in outs),
        in_specs=[SM, SM] + [VM] * (len(operands) - 2),
        out_specs=tuple(VM for _ in outs),
        scratch_shapes=[pltpu.VMEM(*s) for s in scratch] + [pltpu.SemaphoreType.DMA(s) for s in sems],
        compiler_params=pltpu.CompilerParams(vmem_limit_bytes=VMEM_BYTES, collective_id=0, has_side_effects=True),
        name="whole",
    )(*operands)


def one_hot(rows):
    out = np.zeros((rows.size, rows.size), np.float32)
    out[np.arange(rows.size), rows] = 1.0
    return jnp.asarray(out, BF)


def body(grid_field, order_slots, mix_weight, degree_gain, cotangent):
    d, s, j = np.meshgrid(np.arange(32), np.arange(4), np.arange(4), indexing="ij")
    perm = one_hot((j * 128 + d * 4 + s).reshape(-1))
    s, e, j = np.meshgrid(np.arange(4), np.arange(16), np.arange(4), indexing="ij")
    turn = one_hot((e * 16 + s * 4 + j).reshape(-1))
    theta = math.pi * (np.arange(NLAT) + 0.5) / NLAT
    cosv = jnp.asarray(np.cos(theta).reshape(4, 128), F32)
    logsin = jnp.asarray(np.log(np.sin(theta)).reshape(4, 128), F32)
    band = jnp.asarray(np.repeat(np.sin(theta).reshape(128, JL), CL, axis=1), F32)
    sine_col = jnp.asarray(np.repeat(np.sin(theta).reshape(NLAT, 1), 512, axis=1), F32)
    n = np.arange(1, MODES)
    logs = jnp.asarray(np.concatenate([[0.0], np.cumsum(np.log((2.0 * n - 1.0) / (2.0 * n)))]), F32)
    x = jnp.transpose(grid_field, (1, 0, 2)).reshape(JL * CL, NLON)
    cot = jnp.transpose(cotangent, (1, 0, 2)).reshape(JL * CL, NLON)
    out, spectrum, grad, mix, gain = whole(
        order_slots, logs, order_slots.reshape(1, MODES), cosv, logsin, band, sine_col, perm, turn, mix_weight, degree_gain, x, cot
    )
    out = jnp.transpose(out.reshape(JL, CL, NLON), (1, 0, 2))
    grad = jnp.transpose(grad.reshape(JL, CL, NLON), (1, 0, 2))
    return out, spectrum.reshape(4, 2, CL, MODES), grad, mix, gain


def solution(mesh):
    placed = (P("ch", "lat", None), P(), P(), P("ch", None), P("ch", "lat", None))
    return jax.shard_map(
        body,
        mesh=mesh,
        in_specs=placed,
        out_specs=(
            P("ch", "lat", None),
            P("lat", None, "ch", None),
            P("ch", "lat", None),
            P(None, "ch"),
            P("ch", None),
        ),
        check_vma=False,
    )
```

time: 228 us -> 157 us (0.69)
  Pallas kernels: 190 us -> 147 us
  between operations: 14.2 us -> 0.67 us
  local copies, waits for them, and re-layouts: 17.7 us -> 9.41 us
  other arithmetic: 5.38 us -> 0 us
    pallas_call x10 -> x1, Pallas kernels: 190 us -> 147 us  [whole(): pl.pallas_call(whole_kernel, out_shape=tuple((jax.ShapeDtypeStruct(*o) fo...]
    all_gather x1 -> x0, local copies, waits for them, and re-layouts: 2.57 us -> none  [body(): lax.all_gather(jnp.concatenate([turned, turned], axis=1), 'ch', axis=0)]
    mul x2 -> x0, local copies, waits for them, and re-layouts: 2.51 us -> none  [body(): weights = (parts * same).reshape(512, 512)]
    reshape x2 -> x0, local copies, waits for them, and re-layouts: 2.39 us -> none  [the longest x1 1.52 us: tables(): order_slots.reshape(MODES, 1)]
  transfers between devices with their start and end apart: 1 -> 0, of which waited for: 0 -> 0; matrix products, arithmetic and copies ran while one was open for 5% -> 0% of each run, Pallas kernels for 23% -> 0%
where the time goes in v2:
time: 157 us
  Pallas kernels  147 us (94%)
  local copies, waits for them, and re-layouts  9.41 us (6%)
    pallas_call x1, Pallas kernels, whole(): pl.pallas_call(whole_kernel, out_shape=tuple((jax.ShapeDtypeStruct(*o) fo...  147 us
    transpose x1, local copies, waits for them, and re-layouts, body(): grad = jnp.transpose(grad.reshape(JL, CL, NLON), (1, 0, 2))  3.79 us

profile of v2, /device:TPU:1, one launch (start us, length us, event | category | flops | bytes accessed | tf_op | source)
XLA Modules:
  0.0 157.0 jit_solution(1899606443071718168)
XLA Ops:
  0.6 0.0 copy-start
  0.6 2.2 %copy.17 = bf16[4,64,1440]{2,1,0:T(8,128)(2,1)} copy(bf16[4,64,1440]{2,0,1:T(4,128)(2,1)} %bitcast.14) | data formatting | bytes 1474560 | tf_op jit(solution)/shard_map/transpose | solution.py:515
  2.9 0.0 copy-done
  2.9 1.0 copy.18
  3.9 146.9 %whole.1 = (bf16[256,1440]{1,0:T(8,128)(2,1)}, bf16[4,128,512]{2,1,0:T(8,128)(2,1)}, bf16[256,1440]{1,0:T(8,128)(2,1)}, f32[256,64]{1,0:T(8,128)}, f32[64,512]{1,0:T(8,128)}) custom-call(s32[512]{0:T(512)} %slots_ref.1, f32[512]{0:T(512)} %constant.20.clone.logs_ref, s32[1,512]{1,0:T(1,128)} %bitcast.19, f32[4,128]{1,0:T(4,128)} %constant.16.clone.cosv_ref, ...), custom_call_target="tpu_custom_call" | custom-call | tf_op jit(solution)/shard_map/whole/pallas_call | solution.py:486
  150.7 0.0 copy-start.2
  150.8 0.0 copy-start.1
  150.8 3.8 %copy_bitcast_fusion = (bf16[64,4,1440]{2,1,0:T(4,128)(2,1)}, bf16[64,4,1440]{2,1,0:T(4,128)(2,1)}) fusion(bf16[4,64,1440]{2,1,0:T(8,128)(2,1)} %bitcast.17, bf16[4,64,1440]{2,1,0:T(8,128)(2,1)} %bitcast.16), kind=kLoop, calls=%fused_computation | loop fusion | bytes 2949120 | tf_op jit(solution)/shard_map/transpose | solution.py:521
  154.6 0.0 copy-done.2
  154.6 0.7 copy.21
  155.3 0.0 copy-done.1
  155.3 0.0 copy-start.3
  155.3 0.8 copy.26
  156.1 0.2 copy-done.3
  156.3 0.7 copy.27
Async XLA Ops:
  0.6 2.2 %copy-start = (bf16[64,4,1440]{2,1,0:T(4,128)(2,1)S(1)}, bf16[64,4,1440]{2,1,0:T(4,128)(2,1)}, u32[]{:S(2)}) copy-start(bf16[64,4,1440]{2,1,0:T(4,128)(2,1)} %param.16) | copy-start | bytes 2211844
  150.7 3.8 %copy-start.2 = (f32[256,64]{1,0:T(8,128)S(1)}, f32[256,64]{1,0:T(8,128)}, u32[]{:S(2)}) copy-start(f32[256,64]{1,0:T(8,128)} %get-tuple-element.18) | copy-start | bytes 196612
  150.8 4.5 %copy-start.1 = (bf16[4,128,512]{2,1,0:T(8,128)(2,1)S(1)}, bf16[4,128,512]{2,1,0:T(8,128)(2,1)}, u32[]{:S(2)}) copy-start(bf16[4,128,512]{2,1,0:T(8,128)(2,1)} %get-tuple-element.11) | copy-start | bytes 1572868
  155.3 1.0 copy-start.3

commit v3 on v2

v3 whole, which is shorter than its diff:
```python
import math

import jax
import jax.numpy as jnp
import numpy as np
from jax import lax
from jax.experimental import pallas as pl
from jax.experimental.pallas import tpu as pltpu
from jax.sharding import PartitionSpec as P

MESH = pl.DeviceIdType.MESH
BF, F32 = jnp.bfloat16, jnp.float32
CL, JL, NLON = 64, 4, 1440
NZ, NY, NC, NX = 8, 8, 2, 4
NLAT, MODES = 512, 512
RENEW = 32
VMEM_BYTES = 56 * 1024 * 1024
NN = (((1,), (0,)), ((), ()))
NT = (((1,), (1,)), ((), ()))
TN = (((0,), (0,)), ((), ()))


def dot(a, b, dims=NN):
    return lax.dot_general(a, b, dims, preferred_element_type=F32)


def half_angle(steps):
    turns = jnp.floor(steps * (1.0 / NLON) + 0.5)
    t = (steps - turns * NLON) * (math.pi / NLON)
    u = t * t
    s = t * (1.0 + u * (-1.0 / 6 + u * (1.0 / 120 + u * (-1.0 / 5040 + u * (1.0 / 362880 + u * (-1.0 / 39916800))))))
    c = 1.0 + u * (-0.5 + u * (1.0 / 24 + u * (-1.0 / 720 + u * (1.0 / 40320 + u * (-1.0 / 3628800 + u * (1.0 / 479001600))))))
    return 1.0 - 2.0 * s * s, 2.0 * s * c


def long_tables(mcol_ref, f_ref):
    def long_rows(i, carry):
        rows = pl.ds(pl.multiple_of(i * 64, 64), 64)
        lower = pl.ds(pl.multiple_of(i * 64 + MODES, 64), 64)
        mc = mcol_ref[rows, :]
        lane = lax.broadcasted_iota(jnp.int32, (64, 128), 1).astype(F32)
        cb, sb = half_angle(mc * lane)
        ca, sa = half_angle(mc * (lane * 128.0))
        cb, sb = cb * math.sqrt(2.0 / NLON), sb * math.sqrt(2.0 / NLON)
        for a in range(12):
            width = min(128, NLON - a * 128)
            cav = jnp.broadcast_to(ca[:, a : a + 1], (64, 128))
            sav = jnp.broadcast_to(sa[:, a : a + 1], (64, 128))
            f_ref[rows, a * 128 : a * 128 + width] = (cav * cb - sav * sb).astype(BF)[:, :width]
            f_ref[lower, a * 128 : a * 128 + width] = (-(sav * cb + cav * sb)).astype(BF)[:, :width]
        return carry

    lax.fori_loop(0, 8, long_rows, 0)


def legendre_start(m, logs, logsin, up_ref, low_ref):
    k = lax.broadcasted_iota(jnp.int32, (MODES, 128), 0).astype(F32)
    degree = k + (m + 1.0)
    upper = jnp.sqrt((4.0 * degree * degree - 1.0) / (degree * degree - m * m))
    below = degree - 1.0
    lower = jnp.sqrt((below * below - m * m) / jnp.maximum(4.0 * below * below - 1.0, 1.0))
    up_ref[...] = upper
    low_ref[...] = upper * lower
    start = 0.5 * (jnp.log(jnp.full((4, 128), m + 0.5, F32)) + logs) + m * logsin
    zero = jnp.zeros((4, 128), F32)
    return zero, zero + 1.0, start


def legendre_steps(first, last, carry, cosv, up_ref, low_ref, raw_ref):
    def block(b, carry):
        previous, current, scale = carry
        factor = jnp.exp(0.5 * scale)
        for offset in range(RENEW):
            step = b * RENEW + offset
            raw_ref[pl.ds(pl.multiple_of(step * 4, 4), 4), :] = current * factor * factor
            ua = jnp.broadcast_to(up_ref[pl.ds(step, 1), :], (4, 128)) * cosv
            lb = jnp.broadcast_to(low_ref[pl.ds(step, 1), :], (4, 128))
            previous, current = current, ua * current - lb * previous
        biggest = jnp.maximum(jnp.abs(previous), jnp.abs(current))
        shift = jnp.log(biggest)
        rescale = jnp.exp(-shift)
        return previous * rescale, current * rescale, scale + shift

    return lax.fori_loop(first, last, block, carry)


def legendre_end(order, raw_ref, l_ref, lt_ref, shift_ref, shift_t_ref):
    live = lax.broadcasted_iota(jnp.int32, (MODES, 128), 0) < MODES - order
    for g in range(4):
        part = raw_ref[pl.ds(g, MODES, stride=4), :]
        part = jnp.where(live, part, 0.0) * math.sqrt(math.pi / NLAT)
        l_ref[:, g * 128 : (g + 1) * 128] = part.astype(BF)
        lt_ref[g * 128 : (g + 1) * 128, :] = jnp.transpose(part).astype(BF)
    k = lax.broadcasted_iota(jnp.int32, (MODES, MODES), 0)
    l = lax.broadcasted_iota(jnp.int32, (MODES, MODES), 1)
    shift_ref[...] = jnp.where(l - k == order, 1.0, 0.0).astype(BF)
    shift_t_ref[...] = jnp.where(k - l == order, 1.0, 0.0).astype(BF)


def pack_blocks(g, perm_ref, s_ref, stage_ref):
    for j in range(JL):
        cols = slice(j * CL, (j + 1) * CL)
        stage_ref[j] = jnp.concatenate([g[:MODES, cols], g[MODES:, cols]], axis=1).astype(BF)
    for g in range(4):
        rows = jnp.concatenate([stage_ref[j, g * 128 : (g + 1) * 128, :] for j in range(JL)], axis=0)
        s_ref[2 * g : 2 * g + 2] = dot(perm_ref[...], rows).astype(BF).reshape(2, 8, 2, 16, 128)


def unpack_blocks(r_ref, perm_ref, half, grid_ref):
    for g in range(4):
        rows = r_ref[2 * g : 2 * g + 2].reshape(512, 128)
        turned = dot(rows, perm_ref[...], TN)
        for j in range(JL):
            piece = turned[:, j * 128 : (j + 1) * 128]
            if half is not None:
                piece = piece * half[:, g * 128 : (g + 1) * 128]
            piece = piece.astype(BF)
            for r in range(2):
                at = r * MODES + g * 128
                grid_ref[j * CL : (j + 1) * CL, at : at + 128] = piece[r * CL : (r + 1) * CL]


CHUNKS = ((0, 384), (384, 384), (768, 384), (1152, 288))


def to_rows(field_ref, rows_ref):
    for j in range(JL):
        rows_ref[j * CL : (j + 1) * CL, :] = field_ref[:, j, :]


def to_field(rows_ref, field_ref):
    for j in range(JL):
        field_ref[:, j, :] = rows_ref[j * CL : (j + 1) * CL, :]


def middle(grid_ref, x_ref, cot_ref, f_ref, y_ref, slope_ref):
    for first, width in CHUNKS:
        cols = slice(first, first + width)
        v = dot(grid_ref[...], f_ref[:, cols])
        cdf = 0.5 * (1.0 + lax.erf(v * (1.0 / math.sqrt(2.0))))
        y_ref[:, cols] = (x_ref[:, cols].astype(F32) + v * cdf).astype(BF)
        slope = cdf + v * jnp.exp(-0.5 * v * v) * (1.0 / math.sqrt(2.0 * math.pi))
        slope_ref[:, cols] = (cot_ref[:, cols].astype(F32) * slope).astype(BF)


def last(grid_ref, cot_ref, f_ref, out_ref):
    for first, width in CHUNKS:
        cols = slice(first, first + width)
        v = dot(grid_ref[...], f_ref[:, cols])
        out_ref[:, cols] = (cot_ref[:, cols].astype(F32) + v).astype(BF)


def mixing_weights(weights, w2_ref):
    zero = jnp.zeros((CL, CL), F32)
    for x in range(NX):
        slab = weights[x * CL : (x + 1) * CL, :]
        pieces = [slab[:, i * CL : (i + 1) * CL] for i in range(NX)]
        top = jnp.concatenate([a for p in pieces for a in (p, zero)], axis=1)
        low = jnp.concatenate([a for p in pieces for a in (zero, p)], axis=1)
        w2_ref[x * 128 : x * 128 + CL, :] = top.astype(BF)
        w2_ref[x * 128 + CL : (x + 1) * 128, :] = low.astype(BF)


def split_gain(gain_ref, out_ref):
    turned = jnp.transpose(gain_ref[...])
    high = turned.astype(BF).astype(F32)
    out_ref[...] = jnp.concatenate([high, turned - high], axis=1).astype(BF)


def gain_rows(shift_ref, garr_ref, rows_ref):
    both = dot(shift_ref[...], flat(garr_ref))
    for x in range(NX):
        row = both[:, x * 128 : x * 128 + CL] + both[:, x * 128 + CL : (x + 1) * 128]
        rows_ref[:, x * 128 : (x + 1) * 128] = jnp.concatenate([row, row], axis=1)


def gain_sums(grad_ref, mixed_ref, shift_t_ref, sums_ref):
    parts = []
    for x in range(NX):
        cols = slice(x * 128, (x + 1) * 128)
        prod = grad_ref[:, cols] * mixed_ref[:, cols].astype(F32)
        prod = prod[:, :CL] + prod[:, CL:]
        high = prod.astype(BF).astype(F32)
        parts.append(jnp.concatenate([high, prod - high], axis=1).astype(BF))
    both = dot(shift_t_ref[...], jnp.concatenate(parts, axis=1))
    for x in range(NX):
        row = both[:, x * 128 : x * 128 + CL] + both[:, x * 128 + CL : (x + 1) * 128]
        sums_ref[x, 128:384, :] = jnp.concatenate([row[:256], row[256:]], axis=1).astype(BF)


def mix_sums(coeff_t_ref, pre_ref, sums_ref):
    mix = dot(coeff_t_ref[...], pre_ref[...])
    for x in range(NX):
        blocks = []
        for i in range(NX):
            a = mix[i * 128 : i * 128 + CL, x * 128 : x * 128 + CL]
            b = mix[i * 128 + CL : (i + 1) * 128, x * 128 + CL : (x + 1) * 128]
            blocks.append(a + b)
        low = jnp.concatenate([blocks[0], blocks[1]], axis=0)
        high = jnp.concatenate([blocks[2], blocks[3]], axis=0)
        sums_ref[x, 0:128, :] = jnp.concatenate([low, high], axis=1).astype(BF)


def flat(q_ref):
    return jnp.concatenate([q_ref[x] for x in range(NX)], axis=1)


def split_lanes(value, scale, ref):
    for x in range(NX):
        part = value[:, x * 128 : (x + 1) * 128]
        ref[x] = (part if scale is None else part * scale).astype(BF)


class Place:
    def __init__(self):
        lat = lax.axis_index("lat")
        self.x = lax.axis_index("ch")
        self.c = lax.rem(lat, 2)
        self.y = lax.rem(lax.div(lat, 2), 8)
        self.z = lax.div(lat, 16)
        self.major = jnp.where(self.c == 0, self.z, self.y)

    def at(self, z=None, y=None, c=None, x=None):
        z, y = (self.z if z is None else z), (self.y if y is None else y)
        c, x = (self.c if c is None else c), (self.x if x is None else x)
        return ((z * 8 + y) * 2 + c, x)


NEAR = (0, 1, 7, 2, 6, 3, 5, 4)
FAR = (4, 3, 5, 2, 6, 1, 7, 0)


def around(value, step, count):
    return lax.rem(value + step, count)


def send(src, dst, ssem, rsem, target):
    pltpu.make_async_remote_copy(
        src_ref=src, dst_ref=dst, send_sem=ssem, recv_sem=rsem, device_id=target, device_id_type=MESH
    ).start()


def settle(view, sem):
    pltpu.make_async_copy(view, view, sem).wait()


def greet(me):
    barrier = pltpu.get_barrier_semaphore()
    other = 1 - me.c
    targets = [me.at(c=other)]
    for o in range(1, 8):
        targets += [me.at(y=around(me.y, o, 8)), me.at(z=around(me.z, o, 8))]
        targets += [me.at(y=around(me.y, o, 8), c=other), me.at(z=around(me.z, o, 8), c=other)]
    for o in range(1, 4):
        targets.append(me.at(x=around(me.x, o, 4)))
    for target in targets:
        pl.semaphore_signal(barrier, inc=1, device_id=target, device_id_type=MESH)
    return len(targets)


def orders_first(me, s_ref, ta_ref, tb_ref, ssem, rsem, lsem):
    pltpu.make_async_copy(s_ref.at[:, me.y, 0], ta_ref.at[me.y], lsem.at[0]).start()
    pltpu.make_async_copy(s_ref.at[me.z, :, 1], tb_ref.at[me.z], lsem.at[1]).start()
    for o in FAR[:7]:
        y, z = around(me.y, o, 8), around(me.z, o, 8)
        send(s_ref.at[:, y, 0], ta_ref.at[me.y], ssem.at[0], rsem.at[0], me.at(y=y))
        send(s_ref.at[z, :, 1], tb_ref.at[me.z], ssem.at[1], rsem.at[1], me.at(z=z))


def orders_second(me, ta_ref, tb_ref, r_ref, ssem, gsem, rsem, lsem):
    settle(ta_ref.at[0], lsem.at[0])
    settle(ta_ref.at[0:7], rsem.at[0])
    settle(tb_ref.at[0], lsem.at[1])
    settle(tb_ref.at[0:7], rsem.at[1])
    here_a, here_b = r_ref.at[me.z, :, me.c], r_ref.at[me.y, :, me.c]
    to_a, to_b = 2 + me.c, 3 - me.c

    @pl.when(me.c == 0)
    def _():
        pltpu.make_async_copy(ta_ref.at[:, me.z], here_a, lsem.at[2]).start()
        send(tb_ref.at[:, me.y], here_b, ssem.at[3], gsem.at[me.y], me.at(c=1))

    @pl.when(me.c == 1)
    def _():
        pltpu.make_async_copy(tb_ref.at[:, me.y], here_b, lsem.at[2]).start()
        send(ta_ref.at[:, me.z], here_a, ssem.at[3], gsem.at[me.z], me.at(c=0))

    for o in NEAR[1:]:
        y, z = around(me.y, o, 8), around(me.z, o, 8)
        send(ta_ref.at[:, z], here_a, ssem.at[to_a], gsem.at[me.z], me.at(z=z, c=0))
        send(tb_ref.at[:, y], here_b, ssem.at[to_b], gsem.at[me.y], me.at(y=y, c=1))


def orders_third(me, r_ref, perm_ref, p_ref, q_ref, gsem, lsem, xs, xr):
    for o in NEAR:
        g = around(me.major, o, 8)
        if o == 0:
            settle(r_ref.at[0, :, 0], lsem.at[2])
            settle(r_ref.at[0, :, 0], gsem.at[g])
        else:
            settle(r_ref.at[0], gsem.at[g])
        out = dot(perm_ref[...], r_ref[g].reshape(256, 128)).astype(BF)
        at = pl.ds(pl.multiple_of(g * 64, 64), 64)
        for s in range(4):
            p_ref[s, at, :] = out[s * 64 : (s + 1) * 64]
        for k in (2, 1, 3):
            x = around(me.x, k, 4)
            send(p_ref.at[x, at], q_ref.at[me.x, at], xs, xr, me.at(x=x))
        q_ref[me.x, at, :] = p_ref[me.x, at, :]


def lat_sent(ta_ref, ssem):
    settle(ta_ref.at[0:7], ssem.at[0])
    settle(ta_ref.at[0:7], ssem.at[1])
    settle(ta_ref.at[0:7], ssem.at[2])
    settle(ta_ref, ssem.at[3])


def grid_first(me, ret_ref, p_ref, xs, gsem):
    for o in FAR:
        g = around(me.major, o, 8)
        at = pl.ds(pl.multiple_of(g * 64, 64), 64)
        for k in (2, 1, 3):
            x = around(me.x, k, 4)
            send(ret_ref.at[x, at], p_ref.at[me.x, at], xs, gsem.at[g], me.at(x=x))
    p_ref[me.x] = ret_ref[me.x]


def grid_second(me, p_ref, perm_ref, s_ref, t_ref, ssem, rsem, gsem, lsem):
    here = t_ref.at[me.c, me.major]
    for o in FAR:
        g = around(me.major, o, 8)
        at = pl.ds(pl.multiple_of(g * 64, 64), 64)
        settle(p_ref.at[0:3, 0:64], gsem.at[g])
        rows = jnp.concatenate([p_ref[s, at, :] for s in range(4)], axis=0)
        s_ref[g] = dot(perm_ref[...], rows, TN).astype(BF).reshape(8, 2, 16, 128)
        z, y = jnp.where(me.c == 0, g, me.z), jnp.where(me.c == 0, me.y, g)
        other = 1 - me.c
        send(s_ref.at[g, :, other], here, ssem.at[3], rsem.at[3], me.at(z=z, y=y, c=other))
        if o == 0:
            pltpu.make_async_copy(s_ref.at[g, :, me.c], here, lsem.at[0]).start()
        else:
            send(s_ref.at[g, :, me.c], here, ssem.at[2], rsem.at[2], me.at(z=z, y=y))


def grid_third(me, t_ref, r_ref, ssem, rsem, lsem):
    settle(t_ref.at[0, 0], lsem.at[0])
    settle(t_ref.at[0, 0:7], rsem.at[2])
    settle(t_ref.at[0], rsem.at[3])
    here_a, here_b = r_ref.at[:, me.y, 0], r_ref.at[me.z, :, 1]
    for o in FAR[:7]:
        y, z = around(me.y, o, 8), around(me.z, o, 8)
        send(t_ref.at[0, :, y], here_a, ssem.at[0], rsem.at[0], me.at(y=y))
        send(t_ref.at[1, :, z], here_b, ssem.at[1], rsem.at[1], me.at(z=z))
    pltpu.make_async_copy(t_ref.at[0, :, me.y], here_a, lsem.at[1]).start()
    pltpu.make_async_copy(t_ref.at[1, :, me.z], here_b, lsem.at[2]).start()


def grid_end(t_ref, rsem, lsem):
    settle(t_ref.at[0, 0], lsem.at[1])
    settle(t_ref.at[0, 0], lsem.at[2])
    settle(t_ref.at[0, 0:7], rsem.at[0])
    settle(t_ref.at[0, 0:7], rsem.at[1])


def x_start(me, src_ref, dst_ref, ssem, rsem, lsem):
    for o in (2, 1, 3):
        x = around(me.x, o, 4)
        send(src_ref.at[x], dst_ref.at[me.x], ssem, rsem, me.at(x=x))
    pltpu.make_async_copy(src_ref.at[me.x], dst_ref.at[me.x], lsem).start()


def x_end(dst_ref, rsem, lsem):
    settle(dst_ref.at[0], lsem)
    settle(dst_ref.at[0:3], rsem)


def whole_kernel(
    slots_ref, logs_ref, mrow_ref, cosv_ref, logsin_ref, band_ref, sine_ref, perm_ref, turn_ref, w_ref, gain_ref, xfield_ref, cfield_ref,
    yfield_ref, spectrum_ref, out_ref, mix_ref, ggain_ref,
    x_ref, cot_ref, y_ref,
    f_ref, mcol_ref, up_ref, low_ref, raw_ref, l_ref, lt_ref, shift_ref, shift_t_ref, w2_ref, w2t_ref, gsend_ref, garr_ref, grows_ref,
    stage_ref, grid_ref, slope_ref, coeff_ref, coeff_t_ref, mixed_ref, flat_ref, pre_ref, grad_ref, spec_ref, ret_ref, ret2_ref,
    s_refs, ta_refs, tb_refs, t_refs, r_refs, p_refs, q_refs,
    sums_ref, v_ref, own_ref, ybuf_ref, piece_ref, zbuf_ref, fin_ref, total_ref,
    ssem, rsem, gsem, lsem, xs, xr, xl, gs, gr,
):
    me = Place()
    other = 1 - me.c
    peers = greet(me)
    lat = lax.axis_index("lat")
    order = slots_ref[lat * NX + me.x]
    m = order.astype(F32)
    mrow = mrow_ref[...]
    half_row = jnp.where(mrow == 0, 0.5, 1.0)
    mcol_ref[...] = jnp.transpose(jnp.broadcast_to(mrow.astype(F32), (128, MODES)))
    split_gain(gain_ref, gsend_ref)
    long_tables(mcol_ref, f_ref)

    sines = band_ref[pl.ds(lat, 1), :]
    to_rows(xfield_ref, x_ref)
    g = dot(f_ref[...], x_ref[...], NT) * sines
    pack_blocks(g, perm_ref, s_refs.at[0], stage_ref)
    pl.semaphore_wait(pltpu.get_barrier_semaphore(), peers)

    def xlinks(i):
        return xs.at[i], xr.at[i], xl.at[i]

    def begin(i):
        orders_first(me, s_refs.at[i], ta_refs.at[i // 2], tb_refs.at[i // 2], ssem.at[i], rsem.at[i], lsem.at[i])

    def carry_on(i):
        refs = ta_refs.at[i // 2], tb_refs.at[i // 2], r_refs.at[i]
        orders_second(me, *refs, ssem.at[i], gsem.at[i], rsem.at[i], lsem.at[i])
        refs = r_refs.at[i], turn_ref, p_refs.at[i], q_refs.at[i // 2]
        orders_third(me, *refs, gsem.at[i], lsem.at[i], xs.at[i], xr.at[i])

    def back_on(i):
        refs = p_refs.at[i], turn_ref, s_refs.at[i], t_refs.at[i // 2]
        grid_second(me, *refs, ssem.at[i], rsem.at[i], gsem.at[i], lsem.at[i])

    def back_out(i):
        grid_third(me, t_refs.at[i // 2], r_refs.at[i], ssem.at[i], rsem.at[i], lsem.at[i])

    def back_end(i):
        grid_end(t_refs.at[i // 2], rsem.at[i], lsem.at[i])

    begin(0)
    for o in range(1, 4):
        x = around(me.x, o, 4)
        send(gsend_ref, garr_ref.at[me.x], xs.at[6], xr.at[6], me.at(x=x))
    garr_ref[me.x] = gsend_ref[...]
    to_rows(cfield_ref, cot_ref)
    weights = w_ref[...].astype(F32)
    mixing_weights(weights, w2_ref)
    mixing_weights(jnp.transpose(weights), w2t_ref)
    carry = legendre_start(m, logs_ref[order], logsin_ref[me.c], up_ref, low_ref)
    legendre_steps(0, MODES // RENEW, carry, cosv_ref[me.c], up_ref, low_ref, raw_ref)
    legendre_end(order, raw_ref, l_ref, lt_ref, shift_ref, shift_t_ref)
    carry_on(0)
    settle(garr_ref.at[0:3], xr.at[6])
    gain_rows(shift_ref, garr_ref, grows_ref)
    settle(q_refs.at[0, 0:3], xr.at[0])

    coeff_ref[...] = dot(l_ref[...], flat(q_refs.at[0])).astype(BF)
    mixed_ref[...] = dot(coeff_ref[...], w2_ref[...]).astype(BF)
    flat_ref[...] = (mixed_ref[...].astype(F32) * grows_ref[...]).astype(BF)
    split_lanes(dot(lt_ref[...], flat_ref[...]), None, ret_ref)
    grid_first(me, ret_ref, p_refs.at[1], xs.at[1], gsem.at[1])
    back_on(1)
    back_out(1)
    for x in range(NX):
        cols = slice(x * 128, (x + 1) * 128)
        spec_ref[x] = jnp.transpose(flat_ref[:, cols].astype(F32)).astype(BF)
        coeff_t_ref[cols, :] = jnp.transpose(coeff_ref[:, cols].astype(F32)).astype(BF)
    x_start(me, spec_ref, spectrum_ref, *xlinks(4))
    back_end(1)

    unpack_blocks(r_refs.at[1], perm_ref, half_row, grid_ref)
    middle(grid_ref, x_ref, cot_ref, f_ref, y_ref, slope_ref)
    mcol = mcol_ref[...]
    half_col = jnp.where(jnp.concatenate([mcol, mcol], axis=1) == 0.0, 0.5, 1.0)
    half_col = jnp.concatenate([half_col, half_col], axis=0)
    g = dot(f_ref[...], slope_ref[...], NT) * half_col
    pack_blocks(g, perm_ref, s_refs.at[2], stage_ref)
    begin(2)
    to_field(y_ref, yfield_ref)
    carry_on(2)
    settle(q_refs.at[1, 0:3], xr.at[2])

    grad_ref[...] = dot(l_ref[...], flat(q_refs.at[1]))
    pre_ref[...] = (grad_ref[...] * grows_ref[...]).astype(BF)
    back = dot(pre_ref[...], w2t_ref[...]).astype(BF)
    split_lanes(dot(lt_ref[...], back), sine_ref[me.c], ret2_ref)
    grid_first(me, ret2_ref, p_refs.at[3], xs.at[3], gsem.at[3])
    gain_sums(grad_ref, mixed_ref, shift_t_ref, sums_ref)
    mix_sums(coeff_t_ref, pre_ref, sums_ref)
    x_start(me, sums_ref, v_ref, *xlinks(5))
    back_on(3)
    back_out(3)
    x_end(v_ref, xr.at[5], xl.at[5])
    own_ref[...] = sum(v_ref[x].astype(F32) for x in range(NX)).reshape(2, 8, 24, 128)
    for o in FAR:
        y = around(me.y, o, 8)
        if o > 0:
            send(own_ref.at[me.c, y], ybuf_ref.at[me.c, me.y], gs.at[0], gr.at[0], me.at(y=y))
        send(own_ref.at[other, y], ybuf_ref.at[me.c, me.y], gs.at[1], gr.at[1], me.at(y=y, c=other))
    ybuf_ref[me.c, me.y] = own_ref[me.c, me.y]
    settle(ybuf_ref.at[0, 0:7], gr.at[0])
    settle(ybuf_ref.at[0], gr.at[1])
    piece_ref[...] = jnp.sum(ybuf_ref[0] + ybuf_ref[1], axis=0)
    for o in range(1, 8):
        z = around(me.z, o, 8)
        send(piece_ref, zbuf_ref.at[me.z], gs.at[2], gr.at[2], me.at(z=z))
    zbuf_ref[me.z] = piece_ref[...]
    settle(zbuf_ref.at[0:7], gr.at[2])
    fin_ref[...] = jnp.sum(zbuf_ref[...], axis=0)
    for o in range(8):
        y = around(me.y, o, 8)
        if o > 0:
            send(fin_ref, total_ref.at[me.c, me.y], gs.at[3], gr.at[3], me.at(y=y))
        send(fin_ref, total_ref.at[me.c, me.y], gs.at[4], gr.at[4], me.at(y=y, c=other))
    total_ref[me.c, me.y] = fin_ref[...]
    back_end(3)

    unpack_blocks(r_refs.at[3], perm_ref, None, grid_ref)
    last(grid_ref, cot_ref, f_ref, out_ref)
    settle(total_ref.at[0, 0:7], gr.at[3])
    settle(total_ref.at[0], gr.at[4])
    mix = total_ref[0].reshape(192, 128)[0:128] * (1.0 / MODES)
    mix_ref[...] = jnp.transpose(jnp.concatenate([mix[:, :CL], mix[:, CL:]], axis=0))
    gain = jnp.concatenate([total_ref[0].reshape(192, 128)[128:192], total_ref[1].reshape(192, 128)], axis=0)
    gain = jnp.concatenate([gain[:, :CL], gain[:, CL:]], axis=0) * (1.0 / math.sqrt(MODES))
    ggain_ref[...] = jnp.transpose(gain)

    for i in range(4):
        lat_sent(ta_refs.at[0], ssem.at[i])
    x_end(spectrum_ref, xr.at[4], xl.at[4])
    for i in range(5):
        settle(p_refs.at[0, 0:3], xs.at[i])
    settle(v_ref.at[0:3], xs.at[5])
    settle(garr_ref.at[0:3], xs.at[6])
    settle(ybuf_ref.at[0, 0:7], gs.at[0])
    settle(ybuf_ref.at[0], gs.at[1])
    settle(zbuf_ref.at[0:7], gs.at[2])
    settle(total_ref.at[0, 0:7], gs.at[3])
    settle(total_ref.at[0], gs.at[4])


VM = pl.BlockSpec(memory_space=pltpu.VMEM)
SM = pl.BlockSpec(memory_space=pltpu.SMEM)


def whole(*operands):
    scratch = [
        *[((256, NLON), BF)] * 3,
        ((2 * MODES, NLON), BF), ((MODES, 128), F32), ((MODES, 128), F32), ((MODES, 128), F32), ((MODES * 4, 128), F32),
        *[((512, 512), BF)] * 6, ((512, 128), BF), ((4, 512, 128), BF),
        ((512, 512), F32),
        ((4, 512, 128), BF), ((256, 1024), BF), ((256, NLON), BF), ((512, 512), BF), ((512, 512), BF), ((512, 512), BF), ((512, 512), BF),
        ((512, 512), BF), ((512, 512), F32), ((4, 128, 512), BF), ((4, 512, 128), BF), ((4, 512, 128), BF),
        ((4, NZ, NY, NC, 16, 128), BF), ((2, 8, 8, 16, 128), BF), ((2, 8, 8, 16, 128), BF), ((2, 2, 8, 8, 16, 128), BF),
        ((4, NZ, NY, NC, 16, 128), BF),
        ((4, 4, 512, 128), BF), ((2, 4, 512, 128), BF),
        ((4, 384, 128), BF), ((4, 384, 128), BF), ((2, 8, 24, 128), F32), ((2, 8, 24, 128), F32),
        ((24, 128), F32), ((8, 24, 128), F32), ((24, 128), F32), ((2, 8, 24, 128), F32),
    ]
    sems = [(4, 4), (4, 4), (4, 8), (4, 3), (7,), (7,), (7,), (5,), (5,)]
    outs = [((CL, JL, NLON), BF), ((4, 128, 512), BF), ((256, NLON), BF), ((64, 256), F32), ((64, 512), F32)]
    return pl.pallas_call(
        whole_kernel,
        out_shape=tuple(jax.ShapeDtypeStruct(*o) for o in outs),
        in_specs=[SM, SM] + [VM] * (len(operands) - 2),
        out_specs=tuple(VM for _ in outs),
        scratch_shapes=[pltpu.VMEM(*s) for s in scratch] + [pltpu.SemaphoreType.DMA(s) for s in sems],
        compiler_params=pltpu.CompilerParams(vmem_limit_bytes=VMEM_BYTES, collective_id=0, has_side_effects=True),
        name="whole",
    )(*operands)


def finish_kernel(y_in, spec_in, grad_in, mix_in, gain_in, y_out, spec_out, grad_out, mix_out, gain_out):
    y_out[...] = y_in[...]
    spec_out[...] = spec_in[...]
    to_field(grad_in, grad_out)
    mix_out[...] = mix_in[...]
    gain_out[...] = gain_in[...]


def finish(y, spectrum, grad, mix, gain):
    outs = [((CL, JL, NLON), BF), ((4, 128, 512), BF), ((CL, JL, NLON), BF), ((64, 256), F32), ((64, 512), F32)]
    return pl.pallas_call(
        finish_kernel,
        out_shape=tuple(jax.ShapeDtypeStruct(*o) for o in outs),
        in_specs=[VM] * 5,
        out_specs=(VM,) * 5,
        compiler_params=pltpu.CompilerParams(vmem_limit_bytes=VMEM_BYTES),
        name="finish",
    )(y, spectrum, grad, mix, gain)


def one_hot(rows):
    out = np.zeros((rows.size, rows.size), np.float32)
    out[np.arange(rows.size), rows] = 1.0
    return jnp.asarray(out, BF)


def body(grid_field, order_slots, mix_weight, degree_gain, cotangent):
    d, s, j = np.meshgrid(np.arange(32), np.arange(4), np.arange(4), indexing="ij")
    perm = one_hot((j * 128 + d * 4 + s).reshape(-1))
    s, e, j = np.meshgrid(np.arange(4), np.arange(16), np.arange(4), indexing="ij")
    turn = one_hot((e * 16 + s * 4 + j).reshape(-1))
    theta = math.pi * (np.arange(NLAT) + 0.5) / NLAT
    both = np.stack([theta, theta.reshape(8, 8, 8).transpose(1, 0, 2).reshape(-1)])
    cosv = jnp.asarray(np.cos(both).reshape(2, 4, 128), F32)
    logsin = jnp.asarray(np.log(np.sin(both)).reshape(2, 4, 128), F32)
    band = jnp.asarray(np.repeat(np.sin(theta).reshape(128, JL), CL, axis=1), F32)
    sine_col = jnp.asarray(np.repeat(np.sin(both).reshape(2, NLAT, 1), 128, axis=2), F32)
    n = np.arange(1, MODES)
    logs = jnp.asarray(np.concatenate([[0.0], np.cumsum(np.log((2.0 * n - 1.0) / (2.0 * n)))]), F32)
    out, spectrum, grad, mix, gain = whole(
        order_slots, logs, order_slots.reshape(1, MODES), cosv, logsin, band, sine_col, perm, turn,
        mix_weight, degree_gain, grid_field, cotangent,
    )
    out, spectrum, grad, mix, gain = finish(out, spectrum, grad, mix, gain)
    return out, spectrum.reshape(4, 2, CL, MODES), grad, mix.T, gain


def solution(mesh):
    placed = (P("ch", "lat", None), P(), P(), P("ch", None), P("ch", "lat", None))
    return jax.shard_map(
        body,
        mesh=mesh,
        in_specs=placed,
        out_specs=(
            P("ch", "lat", None),
            P("lat", None, "ch", None),
            P("ch", "lat", None),
            P(None, "ch"),
            P("ch", None),
        ),
        check_vma=False,
    )
```

time: 157 us -> 133 us (0.85)
  Pallas kernels: 147 us -> 132 us
  local copies, waits for them, and re-layouts: 9.41 us -> 0 us
    pallas_call x1, Pallas kernels: 147 us -> 129 us  [whole(): pl.pallas_call(whole_kernel, out_shape=tuple((jax.ShapeDtypeStruct(*o) fo...]
    transpose x3 -> x0, local copies, waits for them, and re-layouts: 7.01 us -> none  [the longest x1 3.79 us: body(): grad = jnp.transpose(grad.reshape(JL, CL, NLON), (1, 0, 2))]
    pallas_call x0 -> x1, Pallas kernels: none -> 3.11 us  [finish(): pl.pallas_call(finish_kernel, out_shape=tuple((jax.ShapeDtypeStruct(*o) f...]
    unnamed x11 -> x0, local copies, waits for them, and re-layouts: 2.4 us -> none
where the time goes in v3:
time: 133 us
  Pallas kernels  132 us (99%)
    pallas_call x1, Pallas kernels, whole(): pl.pallas_call(whole_kernel, out_shape=tuple((jax.ShapeDtypeStruct(*o) fo...  129 us
    pallas_call x1, Pallas kernels, finish(): pl.pallas_call(finish_kernel, out_shape=tuple((jax.ShapeDtypeStruct(*o) f...  3.11 us

profile of v3, /device:TPU:1, one launch (start us, length us, event | category | flops | bytes accessed | tf_op | source)
XLA Modules:
  0.0 133.0 jit_solution(7708184964725936892)
XLA Ops:
  0.6 129.3 %whole.1 = (bf16[64,4,1440]{2,1,0:T(4,128)(2,1)}, bf16[4,128,512]{2,1,0:T(8,128)(2,1)}, bf16[256,1440]{1,0:T(8,128)(2,1)}, f32[64,256]{1,0:T(8,128)}, f32[64,512]{1,0:T(8,128)}) custom-call(s32[512]{0:T(512)} %slots_ref.1, f32[512]{0:T(512)} %constant.20.clone.logs_ref, s32[1,512]{1,0:T(1,128)} %bitcast.3, f32[2,4,128]{2,1,0:T(4,128)} %constant.16.clone.cosv_ref, ...), custom_call_target="tpu_custom_call" | custom-call | tf_op jit(solution)/shard_map/whole/pallas_call | solution.py:550
  129.9 3.1 %finish.1 = (bf16[64,4,1440]{2,1,0:T(4,128)(2,1)}, bf16[4,128,512]{2,1,0:T(8,128)(2,1)}, bf16[64,4,1440]{2,1,0:T(4,128)(2,1)}, f32[64,256]{1,0:T(8,128)}, f32[64,512]{1,0:T(8,128)}) custom-call(bf16[64,4,1440]{2,1,0:T(4,128)(2,1)} %get-tuple-element.15.y_in, bf16[4,128,512]{2,1,0:T(8,128)(2,1)} %get-tuple-element.16.spec_in, ...), custom_call_target="tpu_custom_call" | custom-call | tf_op jit(solution)/shard_map/finish/pallas_call | solution.py:571

commit v4 on v3

--- a/solution.py
+++ b/solution.py
@@ -259,36 +259,51 @@
 
 
 def orders_first(me, s_ref, ta_ref, tb_ref, ssem, rsem, lsem):
-    pltpu.make_async_copy(s_ref.at[:, me.y, 0], ta_ref.at[me.y], lsem.at[0]).start()
-    pltpu.make_async_copy(s_ref.at[me.z, :, 1], tb_ref.at[me.z], lsem.at[1]).start()
-    for o in FAR[:7]:
-        y, z = around(me.y, o, 8), around(me.z, o, 8)
-        send(s_ref.at[:, y, 0], ta_ref.at[me.y], ssem.at[0], rsem.at[0], me.at(y=y))
-        send(s_ref.at[z, :, 1], tb_ref.at[me.z], ssem.at[1], rsem.at[1], me.at(z=z))
+    view = s_ref.reshape(4, 2, 4, 2, NC, 16, 128)
+
+    def row(p, y):
+        return view.at[:, p, lax.div(y, 2), lax.rem(y, 2), 0]
+
+    def column(p, z):
+        return view.at[lax.div(z, 2), lax.rem(z, 2), :, p, 1]
+
+    for p in range(2):
+        for o in FAR[:7]:
+            y, z = around(me.y, o, 8), around(me.z, o, 8)
+            send(row(p, y), ta_ref.at[p, me.y], ssem.at[0], rsem.at[p], me.at(y=y))
+            send(column(p, z), tb_ref.at[p, me.z], ssem.at[1], rsem.at[4 + p], me.at(z=z))
+        pltpu.make_async_copy(row(p, me.y), ta_ref.at[p, me.y], lsem.at[p]).start()
+        pltpu.make_async_copy(column(p, me.z), tb_ref.at[p, me.z], lsem.at[3 + p]).start()
 
 
 def orders_second(me, ta_ref, tb_ref, r_ref, ssem, gsem, rsem, lsem):
-    settle(ta_ref.at[0], lsem.at[0])
-    settle(ta_ref.at[0:7], rsem.at[0])
-    settle(tb_ref.at[0], lsem.at[1])
-    settle(tb_ref.at[0:7], rsem.at[1])
     here_a, here_b = r_ref.at[me.z, :, me.c], r_ref.at[me.y, :, me.c]
     to_a, to_b = 2 + me.c, 3 - me.c
-
-    @pl.when(me.c == 0)
-    def _():
-        pltpu.make_async_copy(ta_ref.at[:, me.z], here_a, lsem.at[2]).start()
-        send(tb_ref.at[:, me.y], here_b, ssem.at[3], gsem.at[me.y], me.at(c=1))
-
-    @pl.when(me.c == 1)
-    def _():
-        pltpu.make_async_copy(tb_ref.at[:, me.y], here_b, lsem.at[2]).start()
-        send(ta_ref.at[:, me.z], here_a, ssem.at[3], gsem.at[me.z], me.at(c=0))
-
-    for o in NEAR[1:]:
-        y, z = around(me.y, o, 8), around(me.z, o, 8)
-        send(ta_ref.at[:, z], here_a, ssem.at[to_a], gsem.at[me.z], me.at(z=z, c=0))
-        send(tb_ref.at[:, y], here_b, ssem.at[to_b], gsem.at[me.y], me.at(y=y, c=1))
+    for p in range(2):
+        settle(ta_ref.at[0, 0], lsem.at[p])
+        settle(ta_ref.at[0, 0:7], rsem.at[p])
+        settle(tb_ref.at[0, 0], lsem.at[3 + p])
+        settle(tb_ref.at[0, 0:7], rsem.at[4 + p])
+        for h in range(4):
+            z = lax.rem(lax.div(me.z, 2) + h, 4) * 2 + p
+            y = lax.rem(lax.div(me.y, 2) + h, 4) * 2 + p
+            part_a, part_b = ta_ref.at[p, :, lax.div(z, 2)], tb_ref.at[p, :, lax.div(y, 2)]
+
+            @pl.when(jnp.logical_or(z != me.z, me.c == 1))
+            def _():
+                send(part_a, here_a, ssem.at[to_a], gsem.at[me.z], me.at(z=z, c=0))
+
+            @pl.when(jnp.logical_or(y != me.y, me.c == 0))
+            def _():
+                send(part_b, here_b, ssem.at[to_b], gsem.at[me.y], me.at(y=y, c=1))
+
+            @pl.when(jnp.logical_and(z == me.z, me.c == 0))
+            def _():
+                pltpu.make_async_copy(part_a, here_a, lsem.at[2]).start()
+
+            @pl.when(jnp.logical_and(y == me.y, me.c == 1))
+            def _():
+                pltpu.make_async_copy(part_b, here_b, lsem.at[2]).start()
 
 
 def orders_third(me, r_ref, perm_ref, p_ref, q_ref, gsem, lsem, xs, xr):
@@ -309,11 +324,11 @@
         q_ref[me.x, at, :] = p_ref[me.x, at, :]
 
 
-def lat_sent(ta_ref, ssem):
-    settle(ta_ref.at[0:7], ssem.at[0])
-    settle(ta_ref.at[0:7], ssem.at[1])
-    settle(ta_ref.at[0:7], ssem.at[2])
-    settle(ta_ref, ssem.at[3])
+def lat_sent(t_ref, ssem):
+    settle(t_ref.at[0:7], ssem.at[0])
+    settle(t_ref.at[0:7], ssem.at[1])
+    settle(t_ref.at[0:7], ssem.at[2])
+    settle(t_ref, ssem.at[3])
 
 
 def grid_first(me, ret_ref, p_ref, xs, gsem):
@@ -514,7 +529,7 @@
     ggain_ref[...] = jnp.transpose(gain)
 
     for i in range(4):
-        lat_sent(ta_refs.at[0], ssem.at[i])
+        lat_sent(t_refs.at[0, 0], ssem.at[i])
     x_end(spectrum_ref, xr.at[4], xl.at[4])
     for i in range(5):
         settle(p_refs.at[0, 0:3], xs.at[i])
@@ -539,13 +554,13 @@
         ((512, 512), F32),
         ((4, 512, 128), BF), ((256, 1024), BF), ((256, NLON), BF), ((512, 512), BF), ((512, 512), BF), ((512, 512), BF), ((512, 512), BF),
         ((512, 512), BF), ((512, 512), F32), ((4, 128, 512), BF), ((4, 512, 128), BF), ((4, 512, 128), BF),
-        ((4, NZ, NY, NC, 16, 128), BF), ((2, 8, 8, 16, 128), BF), ((2, 8, 8, 16, 128), BF), ((2, 2, 8, 8, 16, 128), BF),
+        ((4, NZ, NY, NC, 16, 128), BF), ((2, 2, 8, 4, 16, 128), BF), ((2, 2, 8, 4, 16, 128), BF), ((2, 2, 8, 8, 16, 128), BF),
         ((4, NZ, NY, NC, 16, 128), BF),
         ((4, 4, 512, 128), BF), ((2, 4, 512, 128), BF),
         ((4, 384, 128), BF), ((4, 384, 128), BF), ((2, 8, 24, 128), F32), ((2, 8, 24, 128), F32),
         ((24, 128), F32), ((8, 24, 128), F32), ((24, 128), F32), ((2, 8, 24, 128), F32),
     ]
-    sems = [(4, 4), (4, 4), (4, 8), (4, 3), (7,), (7,), (7,), (5,), (5,)]
+    sems = [(4, 4), (4, 6), (4, 8), (4, 5), (7,), (7,), (7,), (5,), (5,)]
     outs = [((CL, JL, NLON), BF), ((4, 128, 512), BF), ((256, NLON), BF), ((64, 256), F32), ((64, 512), F32)]
     return pl.pallas_call(
         whole_kernel,

time: 133 us -> 132 us (level)
  no operation moved by 1% of the time
where the time goes in v4:
time: 132 us
  Pallas kernels  132 us (100%)
    pallas_call x1, Pallas kernels, whole(): pl.pallas_call(whole_kernel, out_shape=tuple((jax.ShapeDtypeStruct(*o) fo...  128 us
    pallas_call x1, Pallas kernels, finish(): pl.pallas_call(finish_kernel, out_shape=tuple((jax.ShapeDtypeStruct(*o) f...  3.11 us

profile of v4, /device:TPU:1, one launch (start us, length us, event | category | flops | bytes accessed | tf_op | source)
XLA Modules:
  0.0 132.2 jit_solution(6672144474830310870)
XLA Ops:
  0.6 128.5 %whole.1 = (bf16[64,4,1440]{2,1,0:T(4,128)(2,1)}, bf16[4,128,512]{2,1,0:T(8,128)(2,1)}, bf16[256,1440]{1,0:T(8,128)(2,1)}, f32[64,256]{1,0:T(8,128)}, f32[64,512]{1,0:T(8,128)}) custom-call(s32[512]{0:T(512)} %slots_ref.1, f32[512]{0:T(512)} %constant.20.clone.logs_ref, s32[1,512]{1,0:T(1,128)} %bitcast.3, f32[2,4,128]{2,1,0:T(4,128)} %constant.16.clone.cosv_ref, ...), custom_call_target="tpu_custom_call" | custom-call | tf_op jit(solution)/shard_map/whole/pallas_call | solution.py:565
  129.1 3.1 %finish.1 = (bf16[64,4,1440]{2,1,0:T(4,128)(2,1)}, bf16[4,128,512]{2,1,0:T(8,128)(2,1)}, bf16[64,4,1440]{2,1,0:T(4,128)(2,1)}, f32[64,256]{1,0:T(8,128)}, f32[64,512]{1,0:T(8,128)}) custom-call(bf16[64,4,1440]{2,1,0:T(4,128)(2,1)} %get-tuple-element.15.y_in, bf16[4,128,512]{2,1,0:T(8,128)(2,1)} %get-tuple-element.16.spec_in, ...), custom_call_target="tpu_custom_call" | custom-call | tf_op jit(solution)/shard_map/finish/pallas_call | solution.py:586

commit v5 on v4

--- a/solution.py
+++ b/solution.py
@@ -576,21 +576,27 @@
 def finish_kernel(y_in, spec_in, grad_in, mix_in, gain_in, y_out, spec_out, grad_out, mix_out, gain_out):
     y_out[...] = y_in[...]
     spec_out[...] = spec_in[...]
-    to_field(grad_in, grad_out)
+    for j in range(JL):
+        grad_out[:, j, :] = grad_in[j]
     mix_out[...] = mix_in[...]
     gain_out[...] = gain_in[...]
 
 
 def finish(y, spectrum, grad, mix, gain):
     outs = [((CL, JL, NLON), BF), ((4, 128, 512), BF), ((CL, JL, NLON), BF), ((64, 256), F32), ((64, 512), F32)]
+    field_part = pl.BlockSpec((16, JL, NLON), lambda i: (i, 0, 0))
+    spec_part = pl.BlockSpec((1, 128, 512), lambda i: (i, 0, 0))
+    mix_part = pl.BlockSpec((16, 256), lambda i: (i, 0))
+    gain_part = pl.BlockSpec((16, 512), lambda i: (i, 0))
     return pl.pallas_call(
         finish_kernel,
         out_shape=tuple(jax.ShapeDtypeStruct(*o) for o in outs),
-        in_specs=[VM] * 5,
-        out_specs=(VM,) * 5,
+        grid=(4,),
+        in_specs=[field_part, spec_part, pl.BlockSpec((JL, 16, NLON), lambda i: (0, i, 0)), mix_part, gain_part],
+        out_specs=(field_part, spec_part, field_part, mix_part, gain_part),
         compiler_params=pltpu.CompilerParams(vmem_limit_bytes=VMEM_BYTES),
         name="finish",
-    )(y, spectrum, grad, mix, gain)
+    )(y, spectrum, grad.reshape(JL, CL, NLON), mix, gain)
 
 
 def one_hot(rows):

time: 132 us -> 133 us (level)
  no operation moved by 1% of the time
where the time goes in v5:
time: 133 us
  Pallas kernels  132 us (99%)
    pallas_call x1, Pallas kernels, whole(): pl.pallas_call(whole_kernel, out_shape=tuple((jax.ShapeDtypeStruct(*o) fo...  128 us
    pallas_call x1, Pallas kernels, finish(): pl.pallas_call(finish_kernel, out_shape=tuple((jax.ShapeDtypeStruct(*o) f...  3.81 us

profile of v5, /device:TPU:1, one launch (start us, length us, event | category | flops | bytes accessed | tf_op | source)
XLA Modules:
  0.0 133.1 jit_solution(13816027495550375864)
XLA Ops:
  0.6 128.5 %whole.1 = (bf16[64,4,1440]{2,1,0:T(4,128)(2,1)}, bf16[4,128,512]{2,1,0:T(8,128)(2,1)}, bf16[256,1440]{1,0:T(8,128)(2,1)}, f32[64,256]{1,0:T(8,128)}, f32[64,512]{1,0:T(8,128)}) custom-call(s32[512]{0:T(512)} %slots_ref.1, f32[512]{0:T(512)} %constant.20.clone.logs_ref, s32[1,512]{1,0:T(1,128)} %bitcast.5, f32[2,4,128]{2,1,0:T(4,128)} %constant.16.clone.cosv_ref, ...), custom_call_target="tpu_custom_call" | custom-call | tf_op jit(solution)/shard_map/whole/pallas_call | solution.py:565
  129.1 3.8 %finish.1 = (bf16[64,4,1440]{2,1,0:T(4,128)(2,1)}, bf16[4,128,512]{2,1,0:T(8,128)(2,1)}, bf16[64,4,1440]{2,1,0:T(4,128)(2,1)}, f32[64,256]{1,0:T(8,128)}, f32[64,512]{1,0:T(8,128)}) custom-call(bf16[64,4,1440]{2,1,0:T(4,128)(2,1)} %get-tuple-element.15.y_in, bf16[4,128,512]{2,1,0:T(8,128)(2,1)} %get-tuple-element.16.spec_in, bf16[4,64,1440]{2,1,0:T(8,128)(2,1)} %bitcast.4, ...), custom_call_target="tpu_custom_call" | custom-call | tf_op jit(solution)/shard_map/finish/pallas_call | solution.py:591
